TPU v7x, 128 devices: a whole 4x4x4 slice. The times are simulated.
128 devices in a mesh: dp: 8 (over x, core), seq: 16 (over z, y).
Axes of the slice: x: 4, y: 4, z: 4, core: 2. Of those that a mesh axis runs over, the one named last changes fastest.
Arguments:
- depths: int32 [8, 4096], P('dp', 'seq'), may hold values from 1 to 3, as said below
- owners: int32 [2, 8, 4096], P(None, 'dp', 'seq'), may hold values from 0 to 15, as said below
- cotangent: bfloat16 [2, 8, 4096, 2048], P(None, 'dp', 'seq'), may hold values from -48 to 48
- query_early: bfloat16 [8, 768, 2048], P('dp', 'seq'), may hold values from -20 to 20
- keyval_early: bfloat16 [8, 768, 2, 2048], P('dp', 'seq'), may hold values from -20 to 20
- query_late: bfloat16 [8, 384, 2048], P('dp', 'seq'), may hold values from -20 to 20
- keyval_late: bfloat16 [8, 384, 2, 2048], P('dp', 'seq'), may hold values from -20 to 20
- out_weight: bfloat16 [2048, 2048], replicated, may hold values from -0.125 to 0.125
Outputs:
- dquery_early: bfloat16 [8, 768, 2048], P('dp', 'seq')
- dkeyval_early: bfloat16 [8, 768, 2, 2048], P('dp', 'seq')
- dquery_late: bfloat16 [8, 384, 2048], P('dp', 'seq')
- dkeyval_late: bfloat16 [8, 384, 2, 2048], P('dp', 'seq')
- dweight: float32 [2048, 2048], P(('dp', 'seq'))
Inputs may be any that keep to these rules, and one draw needn't show every extreme that they name: `depths`: A token is active at the earlier recursion when its depth is 2 or more and at the later one when it is 3. Every sequence has exactly 768 tokens active at the earlier recursion and 384 at the later; in each block of 256 positions the count at the later recursion is a multiple of 16 and the count at the earlier one is twice it. owners[0] holds the earlier recursion, owners[1] the later; entries of tokens not active at that recursion carry no meaning. A block of 256 positions sends the same number of its active tokens to every device along seq, at most 4 at the later recursion and 8 at the earlier, and some block sends exactly that many; every device receives exactly 24 and 48 tokens.
All inputs are finite; a program needn't handle non-finite values.
Results may differ from a plain program's by a relative error of at most 0.024.
Values may be sent and summed in bfloat16 or wider, within the bound.
A program may use at most 128 MiB of HBM per device.

v0:
```python
import jax
import jax.numpy as jnp
from jax import lax
from jax.sharding import PartitionSpec as P

HEADS = 16
HEAD_DIM = 128
SLOTS_LATE = 24
PEAK_LATE = 4
SLOTS_EARLY = 48
PEAK_EARLY = 8


def contract_rows(left, right):
    return lax.dot_general(
        left, right, (((0,), (0,)), ((), ())), preferred_element_type=jnp.float32
    )


def encode_places(places):
    shifted = places + 1
    return jnp.stack([shifted // 256, shifted % 256], axis=-1).astype(jnp.bfloat16)


def decode_places(coded):
    digits = coded.astype(jnp.int32)
    return digits[..., 0] * 256 + digits[..., 1] - 1


def pack_rows(active, owner, values, peak, seq_count, first):
    length = active.shape[0]
    flags = active.astype(jnp.int32)
    before = jnp.cumsum(flags) - flags
    target = owner * peak + before // seq_count
    lanes = jnp.arange(seq_count * peak, dtype=jnp.int32)
    select = (target[None, :] == lanes[:, None]) & active[None, :]
    packed = jnp.dot(
        select.astype(jnp.bfloat16), values, preferred_element_type=jnp.float32
    ).astype(jnp.bfloat16)
    positions = first + jnp.arange(length, dtype=jnp.int32)
    anchor = jnp.max(jnp.where(select, positions[None, :], -1), axis=1)
    return (
        packed.reshape(seq_count, peak, values.shape[1]),
        encode_places(anchor.reshape(seq_count, peak)),
    )


def unpack_rows(packed, coded_anchor, slots):
    anchor = decode_places(coded_anchor)
    seq_count, peak = anchor.shape
    valid = anchor >= 0
    counts = jnp.sum(valid.astype(jnp.int32), axis=1)
    offset = jnp.cumsum(counts) - counts
    target = (offset[:, None] + jnp.arange(peak, dtype=jnp.int32)[None, :]).reshape(-1)
    valid = valid.reshape(-1)
    lanes = jnp.arange(slots, dtype=jnp.int32)
    select = (target[None, :] == lanes[:, None]) & valid[None, :]
    rows = jnp.dot(
        select.astype(jnp.bfloat16),
        packed.reshape(seq_count * peak, -1),
        preferred_element_type=jnp.float32,
    ).astype(jnp.bfloat16)
    places = jnp.max(jnp.where(select, anchor.reshape(-1)[None, :], -1), axis=1)
    return (rows, places)


def send_apart(packed, anchor):
    return (
        lax.all_to_all(packed, "seq", split_axis=0, concat_axis=0, tiled=True),
        lax.all_to_all(anchor, "seq", split_axis=0, concat_axis=0, tiled=True),
    )


def recursion_grads(query, keyval, rows_in, places, out_weight):
    slots = query.shape[0]
    score_scale = HEAD_DIM ** (-0.5)
    gathered, gathered_coded = (
        lax.all_gather(keyval, "seq", axis=0, tiled=True),
        lax.all_gather(encode_places(places), "seq", axis=0, tiled=True),
    )
    gathered_places = decode_places(gathered_coded)
    total = gathered.shape[0]
    query_heads = query.reshape(slots, HEADS, HEAD_DIM)
    key_heads = gathered[:, 0].reshape(total, HEADS, HEAD_DIM)
    value_heads = gathered[:, 1].reshape(total, HEADS, HEAD_DIM)
    dout = lax.dot_general(
        rows_in, out_weight, (((1,), (1,)), ((), ())), preferred_element_type=jnp.float32
    ).astype(jnp.bfloat16)
    dout_heads = dout.reshape(slots, HEADS, HEAD_DIM)
    scores = (
        jnp.einsum("qhe,khe->hqk", query_heads, key_heads, preferred_element_type=jnp.float32)
        * score_scale
    )
    visible = gathered_places[None, None, :] <= places[None, :, None]
    scores = jnp.where(visible, scores, -1e30)
    top = jnp.max(scores, axis=2, keepdims=True)
    weights = jnp.exp(scores - top)
    probs = weights / jnp.sum(weights, axis=2, keepdims=True)
    probs_bf = probs.astype(jnp.bfloat16)
    attended = jnp.einsum(
        "hqk,khe->qhe", probs_bf, value_heads, preferred_element_type=jnp.float32
    ).astype(jnp.bfloat16)
    delta = jnp.einsum("qhe,qhe->hq", dout_heads, attended, preferred_element_type=jnp.float32)
    dprobs = jnp.einsum("qhe,khe->hqk", dout_heads, value_heads, preferred_element_type=jnp.float32)
    dscores = (probs * (dprobs - delta[:, :, None])).astype(jnp.bfloat16)
    dquery = (
        jnp.einsum("hqk,khe->qhe", dscores, key_heads, preferred_element_type=jnp.float32)
        * score_scale
    ).astype(jnp.bfloat16)
    dkey = (
        jnp.einsum("hqk,qhe->khe", dscores, query_heads, preferred_element_type=jnp.float32)
        * score_scale
    )
    dvalue = jnp.einsum("hqk,qhe->khe", probs_bf, dout_heads, preferred_element_type=jnp.float32)
    dkeyval = lax.psum_scatter(
        jnp.stack(
            [
                dkey.reshape(lax.axis_size("seq") * slots, HEADS * HEAD_DIM),
                dvalue.reshape(lax.axis_size("seq") * slots, HEADS * HEAD_DIM),
            ],
            axis=1,
        ).astype(jnp.bfloat16),
        "seq",
        scatter_dimension=0,
        tiled=True,
    )
    return (
        attended.reshape(slots, HEADS * HEAD_DIM),
        dquery.reshape(slots, HEADS * HEAD_DIM),
        dkeyval,
    )


def shards(
    depths, owners, cotangent, query_early, keyval_early, query_late, keyval_late, out_weight
):
    seq_count = lax.axis_size("seq")
    length = depths.shape[1]
    first = lax.axis_index("seq") * length
    depth = depths[0]
    early_pack = pack_rows(depth > 1, owners[0, 0], cotangent[0, 0], PEAK_EARLY, seq_count, first)
    late_pack = pack_rows(depth > 2, owners[1, 0], cotangent[1, 0], PEAK_LATE, seq_count, first)
    early_recv = send_apart(early_pack[0], early_pack[1])
    late_recv = send_apart(late_pack[0], late_pack[1])
    early_rows, early_places = unpack_rows(early_recv[0], early_recv[1], SLOTS_EARLY)
    late_rows, late_places = unpack_rows(late_recv[0], late_recv[1], SLOTS_LATE)
    early_attn, early_dquery, early_dkeyval = recursion_grads(
        query_early[0], keyval_early[0], early_rows, early_places, out_weight
    )
    late_attn, late_dquery, late_dkeyval = recursion_grads(
        query_late[0], keyval_late[0], late_rows, late_places, out_weight
    )
    dweight = lax.psum_scatter(
        contract_rows(early_attn, early_rows) + contract_rows(late_attn, late_rows),
        ("dp", "seq"),
        scatter_dimension=0,
        tiled=True,
    )
    return (early_dquery[None], early_dkeyval[None], late_dquery[None], late_dkeyval[None], dweight)


def solution(mesh):
    in_specs = (
        P("dp", "seq"),
        P(None, "dp", "seq"),
        P(None, "dp", "seq", None),
        P("dp", "seq", None),
        P("dp", "seq", None, None),
        P("dp", "seq", None),
        P("dp", "seq", None, None),
        P(),
    )
    out_specs = (
        P("dp", "seq", None),
        P("dp", "seq", None, None),
        P("dp", "seq", None),
        P("dp", "seq", None, None),
        P(("dp", "seq"), None),
    )
    return jax.shard_map(shards, mesh=mesh, in_specs=in_specs, out_specs=out_specs, check_vma=False)
```

profile of v0, /device:TPU:0, one launch (start us, length us, event | category | flops | bytes accessed | tf_op | source)
XLA Modules:
  0.0 1066.5 jit_solution(17766566234681363274)
XLA Ops:
  12.2 8.1 all-to-all-start.2
  22.2 2.4 fusion.2
  27.8 5.7 all-to-all-start
  34.3 21.0 %all-gather.3 = bf16[16,24,2]{1,2,0:T(2,128)(2,1)S(1)} all-gather(bf16[1,24,2]{1,2,0:T(2,128)(2,1)S(1)} %maximum_bitcast_fusion.1), channel_id=1, replica_groups=mesh['dp'=8,'seq'=16] {'seq'}, dimensions={0}, use_global_device_ids=true | all-gather | bytes 1632 | tf_op jit(solution)/shard_map/all_gather | solution.py:79
  55.5 5.2 all-to-all-start.3
  61.6 21.0 %all-gather.2 = bf16[16,48,2]{1,2,0:T(2,128)(2,1)S(1)} all-gather(bf16[1,48,2]{1,2,0:T(2,128)(2,1)S(1)} %maximum_bitcast_fusion), channel_id=1, replica_groups=mesh['dp'=8,'seq'=16] {'seq'}, dimensions={0}, use_global_device_ids=true | all-gather | bytes 3264 | tf_op jit(solution)/shard_map/all_gather | solution.py:79
  83.4 5.3 all-to-all-start.1
  89.0 5.7 convolution_convert_fusion.6
  95.4 3.4 all-to-all-done.1
  99.0 6.0 convolution_convert_fusion.4
  106.6 7.3 copy.153
  117.9 2.3 convolution_convert_fusion.7
  120.2 7.0 copy.164
  127.2 3.2 multiply_reduce_fusion.1
  134.9 8.5 copy.163
  143.4 9.1 pad_maximum_fusion.1
  152.5 16.1 %copy.136 = bf16[1,768,2,2048]{1,3,2,0:T(8,128)(2,1)} copy(bf16[1,768,2,2048]{3,2,0,1:T(2,128)(2,1)} %all-gather.7.cloned.1.call-done) | data formatting | bytes 12582912 | tf_op jit(solution)/shard_map/all_gather | solution.py:78
  168.6 4.9 fusion.83
  174.3 2.2 fusion.85
  176.5 5.0 convolution_convert_fusion.2
  181.4 15.7 %copy.147 = bf16[768,1,2048]{2,1,0:T(2,128)(2,1)} copy(bf16[768,1,2048]{0,2,1:T(8,128)(2,1)} %bitcast.190) | data formatting | bytes 6291456 | tf_op jit(solution)/shard_map/stack;reshape | solution.py:116
  197.2 4.9 multiply_reduce_fusion
  202.0 3.3 multiply_convert_fusion.2
  206.3 2.7 multiply_convert_fusion
  209.0 15.9 %copy.146 = bf16[768,1,2048]{2,1,0:T(2,128)(2,1)} copy(bf16[768,1,2048]{0,2,1:T(8,128)(2,1)} %bitcast.186) | data formatting | bytes 6291456 | tf_op jit(solution)/shard_map/stack;reshape | solution.py:116
  224.9 15.3 %pad_maximum_fusion = bf16[768,2,2048]{2,1,0:T(2,128)(2,1)} fusion(bf16[768,1,2048]{2,1,0:T(2,128)(2,1)} %copy.147, bf16[768,1,2048]{2,1,0:T(2,128)(2,1)} %copy.146), kind=kLoop, calls=%fused_computation.3 | loop fusion | flops 12582912 | bytes 12582912 | tf_op jit(solution)/shard_map/stack | solution.py:116
  241.1 2.4 fusion.34
  243.5 8.8 convolution_add_fusion
  254.9 2.1 fusion.15
  257.7 2.5 fusion.13
  261.0 128.9 %all-reduce.5.cloned.1.call-done = (bf16[768,2,2048]{2,1,0:T(2,128)(2,1)}, bf16[384,2,2048]{2,1,0:T(2,128)(2,1)}) async-done(((bf16[768,2,2048]{2,1,0:T(2,128)(2,1)}, bf16[384,2,2048]{2,1,0:T(2,128)(2,1)}), (bf16[768,2,2048]{2,1,0:T(2,128)(2,1)}, bf16[384,2,2048]{2,1,0:T(2,128)(2,1)})) %all-reduce.5.cloned.1.call-update) | async-done | bytes 9437200
  393.6 666.3 %reduce-scatter.2.cloned.1.call-done = f32[16,2048]{1,0:T(8,128)} async-done(((f32[2048,2048]{1,0:T(8,128)}), f32[16,2048]{1,0:T(8,128)}) %reduce-scatter.2.cloned.1.call-update) | async-done | bytes 131088 | tf_op jit(solution)/shard_map/reduce_scatter | solution.py:153
  (134 shorter events, 33.0 us)
Async XLA Ops:
  7.2 17.4 %copy-start.4 = (bf16[2,1,256,2048]{3,2,1,0:T(8,128)(2,1)S(1)}, bf16[2,1,256,2048]{3,2,1,0:T(8,128)(2,1)}, u32[]{:S(2)}) copy-start(bf16[2,1,256,2048]{3,2,1,0:T(8,128)(2,1)} %param.10) | copy-start | bytes 6291460
  7.2 17.6 %copy-start.17 = (bf16[1,24,2048]{2,1,0:T(8,128)(2,1)S(1)}, bf16[1,24,2048]{2,1,0:T(8,128)(2,1)}, u32[]{:S(2)}) copy-start(bf16[1,24,2048]{2,1,0:T(8,128)(2,1)} %param.13) | copy-start | bytes 294916
  7.2 99.4 %all-gather.9.cloned.1.call-start = ((), (), s32[]{:S(2)}) async-start(), calls=%async_computation.7 | async-start | bytes 3342336 | tf_op jit(solution)/shard_map/all_gather | solution.py:78
  7.9 144.6 %all-gather.7.cloned.1.call-start = ((), (), s32[]{:S(2)}) async-start(), calls=%async_computation.6 | async-start | bytes 6684672 | tf_op jit(solution)/shard_map/all_gather | solution.py:78
  12.2 15.6 %all-to-all-start.2 = ((bf16[16,4,2]{1,2,0:T(2,128)(2,1)}), bf16[16,4,2]{1,2,0:T(2,128)(2,1)S(1)}, u32[]{:S(2)}, u32[]{:S(2)}) async-start(bf16[16,4,2]{1,2,0:T(2,128)(2,1)} %copy.148), calls=%async_computation.2 | async-start | bytes 16384 | tf_op jit(solution)/shard_map/all_to_all | solution.py:70
  27.8 27.7 %all-to-all-start = ((bf16[16,8,2]{1,2,0:T(2,128)(2,1)}), bf16[16,8,2]{1,2,0:T(2,128)(2,1)S(1)}, u32[]{:S(2)}, u32[]{:S(2)}) async-start(bf16[16,8,2]{1,2,0:T(2,128)(2,1)} %copy.131), calls=%async_computation | async-start | bytes 16384 | tf_op jit(solution)/shard_map/all_to_all | solution.py:70
  55.5 27.9 %all-to-all-start.3 = ((bf16[16,4,2048]{2,1,0:T(4,128)(2,1)}), bf16[16,4,2048]{2,1,0:T(4,128)(2,1)S(1)}, u32[]{:S(2)}, u32[]{:S(2)}) async-start(bf16[16,4,2048]{2,1,0:T(4,128)(2,1)} %reshape.697), calls=%async_computation.3 | async-start | bytes 524288 | tf_op jit(solution)/shard_map/all_to_all | solution.py:69
  83.4 15.4 %all-to-all-start.1 = ((bf16[16,8,2048]{2,1,0:T(8,128)(2,1)}), bf16[16,8,2048]{2,1,0:T(8,128)(2,1)S(1)}, u32[]{:S(2)}, u32[]{:S(2)}) async-start(bf16[16,8,2048]{2,1,0:T(8,128)(2,1)} %fusion.2), calls=%async_computation.1 | async-start | bytes 1048576 | tf_op jit(solution)/shard_map/all_to_all | solution.py:69
  88.7 301.2 %all-reduce.5.cloned.1.call-start = ((), (), s32[]{:S(2)}) async-start(), calls=%async_computation.8 | async-start | bytes 18874368
  89.0 5.7 copy-start.7
  94.7 10.4 copy-start.12
  105.1 0.7 copy-start.11
  113.9 2.6 copy-start.9
  115.4 1.1 copy-start
  115.4 2.5 copy-start.13
  116.9 3.3 copy-start.3
  130.4 2.7 copy-start.10
  132.4 0.7 copy-start.5
  173.5 0.8 copy-start.15
  174.3 2.2 copy-start.1
  205.3 1.0 copy-start.2
  240.2 0.9 copy-start.8
  240.2 0.9 copy-start.16
  240.2 819.7 %reduce-scatter.2.cloned.1.call-start = ((), (), s32[]{:S(2)}) async-start(), calls=%async_computation.5 | async-start | bytes 16908288 | tf_op jit(solution)/shard_map/reduce_scatter | solution.py:153
  241.1 2.4 copy-start.14
  252.3 0.7 copy-start.18
  252.3 2.5 copy-start.6
Sparse Core Ops, SparseCore 0:
  10.2 51.9 all-gather.8
  64.2 62.7 all-gather.6
  240.3 149.5 all-reduce.4
  392.8 667.0 reduce-scatter.1
where the time goes:
time: 1070 us
  waiting for transfers between devices  802 us (75%)
  local copies, waits for them, and re-layouts  93 us (9%)
  matrix products  56.5 us (5%)
  blocking collectives  42 us (4%)
  other arithmetic  33.5 us (3%)
  starting transfers between devices  24.5 us (2%)
  between operations  15.5 us (1%)
    reduce_scatter x1, waiting for transfers between devices, shards(): lax.psum_scatter(contract_rows(early_attn, early_rows) + contract_rows(la...  666 us
    unnamed x5, waiting for transfers between devices  130 us
    another operation x4, local copies, waits for them, and re-layouts, recursion_grads(): jnp.stack([dkey.reshape(lax.axis_size('seq') * slots, HEADS * HEAD_DIM),...  47.1 us
    all_gather x2, blocking collectives, recursion_grads(): lax.all_gather(encode_places(places), 'seq', axis=0, tiled=True)  42 us
    another operation x2, other arithmetic, recursion_grads(): jnp.stack([dkey.reshape(lax.axis_size('seq') * slots, HEADS * HEAD_DIM),...  24.4 us
    all_gather x2, local copies, waits for them, and re-layouts, recursion_grads(): lax.all_gather(keyval, 'seq', axis=0, tiled=True)  23.4 us
  transfers between devices with their start and end apart: 8, of which 4 were waited for; matrix products, arithmetic and copies ran while one was open for 9% of the time, Pallas kernels for 0%

commit v1 on v0

v1 whole, which is shorter than its diff:
```python
import jax
import jax.numpy as jnp
from jax import lax
from jax.experimental import pallas as pl
from jax.experimental.pallas import tpu as pltpu
from jax.sharding import PartitionSpec as P

MESH = pl.DeviceIdType.MESH
F32, BF16, I32 = jnp.float32, jnp.bfloat16, jnp.int32

N = 16
DP = 8
E = 128
W = 2048
TOK = 256
NE, NL = 48, 24
NLP = 32
ROWS = NE + NLP
KE, KL = N * NE, N * NL
SCALE = E**-0.5


def dot(a, b):
    return lax.dot_general(a, b, (((1,), (0,)), ((), ())), preferred_element_type=F32)


def dot_nt(a, b):
    return lax.dot_general(a, b, (((1,), (1,)), ((), ())), preferred_element_type=F32)


def dot_tn(a, b):
    return lax.dot_general(a, b, (((0,), (0,)), ((), ())), preferred_element_type=F32)


def iota(shape, dim):
    return lax.broadcasted_iota(I32, shape, dim)


def onehot(mask):
    return jnp.where(mask, 1.0, 0.0).astype(BF16)


def kernel(
    depths, owners, cot, qkv, weight,
    out, dw,
    cotv, wv, rows_send, rows_recv, meta_send, meta_recv, qkv_recv, rows_all,
    dout_send, dout_recv, att_send, att_recv, dqkv_send, part_send, part_recv,
    probs_e, probs_bf_e, ds_e, probs_l, probs_bf_l, ds_l,
    local_sem, send, recv, gsend, grecv,
):
    d = lax.axis_index("dp")
    s = lax.axis_index("seq")
    chip = lax.div(d, 2)
    core = lax.rem(d, 2)
    partner = chip * 2 + 1 - core
    target_dp = lax.div(s, 2)
    parity = lax.rem(s, 2)

    cot_copy = pltpu.make_async_copy(cot, cotv, local_sem.at[0])
    weight_copy = pltpu.make_async_copy(weight, wv, local_sem.at[1])
    cot_copy.start()
    weight_copy.start()

    barrier = pltpu.get_barrier_semaphore()

    def greet(to_dp, to_seq):
        pl.semaphore_signal(barrier, inc=1, device_id=(to_dp, to_seq), device_id_type=MESH)

    def greet_seq(i, _):
        greet(d, lax.rem(s + i, N))
        return 0

    lax.fori_loop(1, N, greet_seq, 0)
    greet(partner, s)
    for i in range(1, 4):
        greet(lax.rem(chip + i, 4) * 2 + core, s)

    def greet_heads(i, _):
        from_dp, from_seq = lax.div(i, 2), 2 * d + lax.rem(i, 2)

        @pl.when(jnp.logical_or(from_dp != d, from_seq != s))
        def _():
            greet(from_dp, from_seq)

        return 0

    lax.fori_loop(0, 2 * DP, greet_heads, 0)

    depth = depths[...]
    active_e, active_l = depth > 1, depth > 2
    owner_e, owner_l = owners[0], owners[1]
    flags = jnp.where(
        iota((16, TOK), 0) < 8,
        jnp.broadcast_to(active_e.astype(F32), (16, TOK)),
        jnp.broadcast_to(active_l.astype(F32), (16, TOK)),
    ).astype(BF16)
    below = onehot(iota((TOK, TOK), 0) < iota((TOK, TOK), 1))
    before = dot(flags, below).astype(I32)
    rank_e, rank_l = before[0:1] >> 4, before[8:9] >> 4
    token = (iota((N, TOK), 1) + 1).astype(F32)
    lane = iota((N, TOK), 0)
    spread_e = jnp.where((lane == owner_e) & active_e, token, 0.0).astype(BF16)
    spread_l = jnp.where((lane == owner_l) & active_l, token, 0.0).astype(BF16)
    line = iota((E, TOK), 0)
    meta_send[0:N] = dot_nt(spread_e, onehot(line == s * 8 + rank_e))
    meta_send[N : 2 * N] = dot_nt(spread_l, onehot(line == s * 4 + rank_l))

    cot_copy.wait()
    line = iota((TOK, TOK), 0)
    base = jnp.where(active_e, owner_e * 16 + rank_e, -64)
    packed = dot(onehot(line == base), cotv[0, :, 0:1024])
    packed += dot(onehot(line == base + 8), cotv[0, :, 1024:2048])
    rows_send[:, :, 0:1024] = packed.reshape(N, 16, 1024).astype(BF16)
    base = jnp.where(active_l, owner_l * 16 + rank_l, -64)
    packed = dot(onehot(line == base), cotv[1, :, 0:512])
    for q in range(1, 4):
        packed += dot(onehot(line == base + 4 * q), cotv[1, :, q * 512 : (q + 1) * 512])
    rows_send[:, :, 1024:1536] = packed.reshape(N, 16, 512).astype(BF16)

    elsewhere = jnp.where(target_dp == d, 0, 1)
    pl.semaphore_wait(barrier, N - 1 + 4 + N - 1 + elsewhere)

    def remote(src, dst, phase, to, sender, to_dp):
        return pltpu.make_async_remote_copy(
            src_ref=src,
            dst_ref=dst,
            send_sem=send.at[phase, to],
            recv_sem=recv.at[phase, sender],
            device_id=(to_dp, to),
            device_id_type=MESH,
        )

    def exchange(phase, src, dst):
        def step(i, _):
            to = lax.rem(s + i, N)
            remote(src(to), dst(s), phase, to, s, d).start()
            return 0

        lax.fori_loop(1, N, step, 0)
        pltpu.make_async_copy(src(s), dst(s), recv.at[phase, s]).start()

    def arrive(phase, src, dst):
        def step(i, _):
            sender = lax.rem(s + i, N)
            remote(src(sender), dst(sender), phase, sender, sender, d).wait_recv()
            return 0

        lax.fori_loop(1, N, step, 0)
        pltpu.make_async_copy(src(s), dst(s), recv.at[phase, s]).wait()

    def sent(phase, src, dst):
        def step(i, _):
            to = lax.rem(s + i, N)
            remote(src(to), dst(s), phase, to, s, d).wait_send()
            return 0

        lax.fori_loop(1, N, step, 0)

    def columns(ref, j):
        return ref.at[:, pl.ds(pl.multiple_of(j * E, E), E)]

    META = (0, lambda j: meta_send, lambda j: meta_recv.at[j])
    ROW = (1, lambda j: rows_send.at[j], lambda j: rows_recv.at[j])
    QKV = (2, lambda j: columns(qkv, j), lambda j: qkv_recv.at[j])
    DOUT = (3, lambda j: columns(dout_send, j), lambda j: dout_recv.at[j])
    GRAD = (4, lambda j: dqkv_send.at[j], lambda j: columns(out, j))
    PART = (5, lambda j: part_send.at[j], lambda j: part_recv.at[j])

    exchange(*META)
    exchange(*ROW)
    exchange(*QKV)

    arrive(*META)
    token_e = jnp.zeros((N, E), F32)
    token_l = jnp.zeros((N, E), F32)
    for j in range(N):
        token_e += meta_recv[j, 0:N]
        token_l += meta_recv[j, N : 2 * N]

    def tables(token, shift, slots, padded):
        peak = 1 << shift
        valid = onehot(token > 0.0)
        src, dst = iota((E, E), 0), iota((E, E), 1)
        offset = dot(valid, onehot((src >> shift) < (dst >> shift)))[0:1].astype(I32)
        in_lane = iota((1, E), 1)
        slot = jnp.where(token[0:1] > 0.0, offset + (in_lane & (peak - 1)), -1)
        select = onehot(iota((padded, E), 0) == slot)
        low = token.astype(BF16)
        high = jnp.where(token > 0.0, (iota((N, E), 1) >> shift).astype(F32), 0.0).astype(BF16)
        cols = dot_nt(select, high) * 256.0 + dot_nt(select, low) - 1.0
        total = N * slots
        mult = 1366 if slots == NE else 2731
        in_row = iota((padded, total), 1)
        tile = onehot(in_row - ((in_row * mult) >> 16) * slots == iota((padded, total), 0))
        wide_high = dot(dot_nt(high, select).astype(BF16), tile)
        wide_low = dot(dot_nt(low, select).astype(BF16), tile)
        in_row = iota((N, total), 1)
        mine = ((in_row * mult) >> 16) == iota((N, total), 0)
        row = jnp.sum(
            jnp.where(mine, wide_high * 256.0 + wide_low - 1.0, 0.0), axis=0, keepdims=True
        )
        src, dst = iota((E, TOK), 0), iota((E, TOK), 1)
        offset = dot(valid, onehot((src >> shift) < (dst >> 4)))[0:1].astype(I32)
        count = dot(valid, onehot((src >> shift) == (dst >> 4)))[0:1].astype(I32)
        in_lane = iota((1, TOK), 1)
        rank = in_lane & (peak - 1)
        slot = jnp.where(rank < count, offset + rank, -1)
        part = (in_lane & 15) >> shift
        return cols, row, slot, part

    cols_e, row_e, slot_e, part_e = tables(token_e, 3, NE, NE)
    cols_l, row_l, slot_l, part_l = tables(token_l, 2, NL, NLP)

    arrive(*ROW)
    for h in range(2):
        pick = onehot((iota((NE, TOK), 0) == slot_e) & (part_e == h))
        got = dot(pick, rows_recv[:, :, 0:1024].reshape(TOK, 1024))
        rows_all[d, 0:NE, h * 1024 : (h + 1) * 1024] = got.astype(BF16)
    for q in range(4):
        pick = onehot((iota((NLP, TOK), 0) == slot_l) & (part_l == q))
        got = dot(pick, rows_recv[:, :, 1024:1536].reshape(TOK, 512))
        rows_all[d, NE:ROWS, q * 512 : (q + 1) * 512] = got.astype(BF16)

    def gather(block, index, to_dp):
        return pltpu.make_async_remote_copy(
            src_ref=rows_all.at[block],
            dst_ref=rows_all.at[block],
            send_sem=gsend.at[index],
            recv_sem=grecv.at[block],
            device_id=(to_dp, s),
            device_id_type=MESH,
        )

    def same_core(i):
        return lax.rem(chip + i, 4) * 2 + core

    gather(d, 0, partner).start()
    for i in (2, 1, 3):
        gather(d, i, same_core(i)).start()

    weight_copy.wait()
    mine = rows_all[d]
    for c in range(8):
        part = dot_nt(mine, wv[c * 256 : (c + 1) * 256, :])
        dout_send[:, c * 256 : (c + 1) * 256] = part.astype(BF16)
    exchange(*DOUT)

    arrive(*QKV)

    def late(ref, first):
        wide = ref[:, first : first + NLP, :].astype(F32)[:, 0:NL, :]
        return wide.reshape(KL, E)

    def softmax(query, key, value, row, col):
        scores = dot_nt(query, key) * SCALE
        scores = jnp.where(row <= col, scores, -1e30)
        top = jnp.max(scores, axis=1, keepdims=True)
        weights = jnp.exp(scores - top)
        probs = weights / jnp.sum(weights, axis=1, keepdims=True)
        probs_bf = probs.astype(BF16)
        return probs, probs_bf, dot(probs_bf, value)

    key_e = qkv_recv[:, NE : 2 * NE, :].reshape(KE, E)
    value_e = qkv_recv[:, 2 * NE : 3 * NE, :].reshape(KE, E)
    for b in range(4):
        query = qkv_recv[4 * b : 4 * b + 4, 0:NE, :].reshape(4 * NE, E)
        col = jnp.concatenate([cols_e[:, o : o + 1] for o in range(4 * b, 4 * b + 4)], axis=0)
        probs, probs_bf, attended = softmax(query, key_e, value_e, row_e, col)
        probs_e[b * 192 : (b + 1) * 192] = probs
        probs_bf_e[b * 192 : (b + 1) * 192] = probs_bf
        att_send[4 * b : 4 * b + 4, 0:NE, :] = attended.reshape(4, NE, E).astype(BF16)
    query_l = late(qkv_recv, 144).astype(BF16)
    key_l = late(qkv_recv, 176).astype(BF16)
    value_l = late(qkv_recv, 208).astype(BF16)
    gap = jnp.zeros((8, NLP - NL, E), F32)
    for b in range(2):
        query = query_l[b * 192 : (b + 1) * 192]
        col = jnp.concatenate([cols_l[0:NL, o : o + 1] for o in range(8 * b, 8 * b + 8)], axis=0)
        probs, probs_bf, attended = softmax(query, key_l, value_l, row_l, col)
        probs_l[b * 192 : (b + 1) * 192] = probs
        probs_bf_l[b * 192 : (b + 1) * 192] = probs_bf
        attended = jnp.concatenate([attended.reshape(8, NL, E), gap], axis=1)
        att_send[8 * b : 8 * b + 8, NE:ROWS, :] = attended.astype(BF16)

    ATT = 6

    def att_copy(to):
        return remote(att_send.at[to], att_recv.at[d, parity], ATT, to, d * 2 + parity, target_dp)

    def att_local():
        return pltpu.make_async_copy(
            att_send.at[s], att_recv.at[d, parity], recv.at[ATT, d * 2 + parity]
        )

    def att_step(i, _):
        att_copy(lax.rem(s + i, N)).start()
        return 0

    lax.fori_loop(1, N, att_step, 0)

    @pl.when(target_dp == d)
    def _():
        att_local().start()

    @pl.when(target_dp != d)
    def _():
        att_copy(s).start()

    for i in (1, 3, 2):
        gather(same_core(i), i, partner).wait_recv()
        gather(same_core(i), 3 + i, partner).start()

    arrive(*DOUT)

    def backward(query, key, value, dout, attended, probs):
        delta = jnp.sum(dout.astype(F32) * attended.astype(F32), axis=1, keepdims=True)
        dprobs = dot_nt(dout, value)
        dscores = (probs * (dprobs - delta)).astype(BF16)
        return dscores, dot(dscores, key) * SCALE

    for b in range(4):
        dout = dout_recv[4 * b : 4 * b + 4, 0:NE, :].reshape(192, E)
        attended = att_send[4 * b : 4 * b + 4, 0:NE, :].reshape(192, E)
        query = None
        dscores, dquery = backward(
            query, key_e, value_e, dout, attended, probs_e[b * 192 : (b + 1) * 192]
        )
        ds_e[b * 192 : (b + 1) * 192] = dscores
        dqkv_send[4 * b : 4 * b + 4, 0:NE, :] = dquery.reshape(4, NE, E).astype(BF16)
    dout_l = late(dout_recv, NE).astype(BF16)
    attended_l = late(att_send, NE)
    for b in range(2):
        dscores, dquery = backward(
            None, key_l, value_l, dout_l[b * 192 : (b + 1) * 192],
            attended_l[b * 192 : (b + 1) * 192], probs_l[b * 192 : (b + 1) * 192]
        )
        ds_l[b * 192 : (b + 1) * 192] = dscores
        dquery = jnp.concatenate([dquery.reshape(8, NL, E), gap], axis=1)
        dqkv_send[8 * b : 8 * b + 8, 144:176, :] = dquery.astype(BF16)
    query_e = qkv_recv[:, 0:NE, :].reshape(KE, E)
    dout_e = dout_recv[:, 0:NE, :].reshape(KE, E)
    for c in range(2):
        dkey = dot_tn(ds_e[:, c * 384 : (c + 1) * 384], query_e) * SCALE
        dqkv_send[8 * c : 8 * c + 8, NE : 2 * NE, :] = dkey.reshape(8, NE, E).astype(BF16)
        dvalue = dot_tn(probs_bf_e[:, c * 384 : (c + 1) * 384], dout_e)
        dqkv_send[8 * c : 8 * c + 8, 2 * NE : 3 * NE, :] = dvalue.reshape(8, NE, E).astype(BF16)
    gap = jnp.zeros((N, NLP - NL, E), F32)
    dkey = dot_tn(ds_l[...], query_l) * SCALE
    dkey = jnp.concatenate([dkey.reshape(N, NL, E), gap], axis=1)
    dqkv_send[:, 176:208, :] = dkey.astype(BF16)
    dvalue = dot_tn(probs_bf_l[...], dout_l)
    dvalue = jnp.concatenate([dvalue.reshape(N, NL, E), gap], axis=1)
    dqkv_send[:, 208:240, :] = dvalue.astype(BF16)
    exchange(*GRAD)

    def att_wait(i, _):
        sender = lax.div(i, 2)
        remote(
            att_send.at[0], att_recv.at[sender, lax.rem(i, 2)], ATT, s, i, target_dp
        ).wait_recv()
        return 0

    lax.fori_loop(0, 2 * DP, att_wait, 0)
    gather(partner, 0, partner).wait_recv()
    for i in (1, 3, 2):
        gather(lax.rem(chip + i, 4) * 2 + 1 - core, i, partner).wait_recv()
    rows = rows_all[...].reshape(DP * ROWS, W)
    for p in range(2):
        attended = att_recv[:, p].reshape(DP * ROWS, E)
        for c in range(4):
            part = dot_tn(attended, rows[:, c * 512 : (c + 1) * 512])
            part_send[8 * p : 8 * p + 8, :, c * 512 : (c + 1) * 512] = part.reshape(
                8, 16, 512
            ).astype(BF16)
    exchange(*PART)
    arrive(*PART)
    total = part_recv[0].astype(F32)
    for j in range(1, N):
        total += part_recv[j].astype(F32)
    dw[...] = total
    arrive(*GRAD)

    for phase in (META, ROW, QKV, DOUT, GRAD, PART):
        sent(*phase)

    def att_sent(i, _):
        att_copy(lax.rem(s + i, N)).wait_send()
        return 0

    lax.fori_loop(1, N, att_sent, 0)

    @pl.when(target_dp != d)
    def _():
        att_copy(s).wait_send()

    for i in range(7):
        gather(d, i, partner).wait_send()


def shards(
    depths, owners, cotangent, query_early, keyval_early, query_late, keyval_late, out_weight
):
    def late(rows):
        return jnp.pad(rows, ((0, NLP - NL), (0, 0)))

    qkv = jnp.concatenate(
        [
            query_early[0],
            keyval_early[0, :, 0],
            keyval_early[0, :, 1],
            late(query_late[0]),
            late(keyval_late[0, :, 0]),
            late(keyval_late[0, :, 1]),
        ],
        axis=0,
    )
    vmem = pl.BlockSpec(memory_space=pltpu.VMEM)
    hbm = pl.BlockSpec(memory_space=pl.ANY)
    grads, dweight = pl.pallas_call(
        kernel,
        out_shape=(
            jax.ShapeDtypeStruct((3 * ROWS, W), BF16),
            jax.ShapeDtypeStruct((N, W), F32),
        ),
        in_specs=[vmem, vmem, hbm, hbm, hbm],
        out_specs=(hbm, vmem),
        scratch_shapes=[
            pltpu.VMEM((2, TOK, W), BF16),
            pltpu.VMEM((W, W), BF16),
            pltpu.VMEM((N, 16, 1536), BF16),
            pltpu.VMEM((N, 16, 1536), BF16),
            pltpu.VMEM((2 * N, E), F32),
            pltpu.VMEM((N, 2 * N, E), F32),
            pltpu.VMEM((N, 3 * ROWS, E), BF16),
            pltpu.VMEM((DP, ROWS, W), BF16),
            pltpu.VMEM((ROWS, W), BF16),
            pltpu.VMEM((N, ROWS, E), BF16),
            pltpu.VMEM((N, ROWS, E), BF16),
            pltpu.VMEM((DP, 2, ROWS, E), BF16),
            pltpu.VMEM((N, 3 * ROWS, E), BF16),
            pltpu.VMEM((N, N, W), BF16),
            pltpu.VMEM((N, N, W), BF16),
            pltpu.VMEM((KE, KE), F32),
            pltpu.VMEM((KE, KE), BF16),
            pltpu.VMEM((KE, KE), BF16),
            pltpu.VMEM((KL, KL), F32),
            pltpu.VMEM((KL, KL), BF16),
            pltpu.VMEM((KL, KL), BF16),
            pltpu.SemaphoreType.DMA((2,)),
            pltpu.SemaphoreType.DMA((7, N)),
            pltpu.SemaphoreType.DMA((7, N)),
            pltpu.SemaphoreType.DMA((7,)),
            pltpu.SemaphoreType.DMA((DP,)),
        ],
        compiler_params=pltpu.CompilerParams(
            collective_id=0, has_side_effects=True, vmem_limit_bytes=56 * 1024 * 1024
        ),
        cost_estimate=pl.CostEstimate(
            flops=3_000_000_000, bytes_accessed=20_000_000, transcendentals=800_000
        ),
        name="rows_attention_weight",
    )(depths, owners[:, 0], cotangent[:, 0], qkv, out_weight)

    def pair(first, second, count):
        return jnp.stack(
            [grads[first : first + count], grads[second : second + count]], axis=1
        )[None]

    return (
        grads[None, 0:NE],
        pair(NE, 2 * NE, NE),
        grads[None, 144 : 144 + NL],
        pair(176, 208, NL),
        dweight,
    )


def solution(mesh):
    in_specs = (
        P("dp", "seq"),
        P(None, "dp", "seq"),
        P(None, "dp", "seq", None),
        P("dp", "seq", None),
        P("dp", "seq", None, None),
        P("dp", "seq", None),
        P("dp", "seq", None, None),
        P(),
    )
    out_specs = (
        P("dp", "seq", None),
        P("dp", "seq", None, None),
        P("dp", "seq", None),
        P("dp", "seq", None, None),
        P(("dp", "seq"), None),
    )
    return jax.shard_map(shards, mesh=mesh, in_specs=in_specs, out_specs=out_specs, check_vma=False)
```

time: 1070 us -> 99 us (0.09)
  waiting for transfers between devices: 802 us -> 0 us
  Pallas kernels: 0 us -> 83.2 us
  local copies, waits for them, and re-layouts: 93 us -> 14.7 us
  matrix products: 56.5 us -> 0 us
  blocking collectives: 42 us -> 0 us
  other arithmetic: 33.5 us -> 0.06 us
  starting transfers between devices: 24.5 us -> 0 us
  between operations: 15.5 us -> 0.71 us
    reduce_scatter x1 -> x0, waiting for transfers between devices: 666 us -> none  [shards(): lax.psum_scatter(contract_rows(early_attn, early_rows) + contract_rows(la...]
    unnamed x5 -> x0, waiting for transfers between devices: 130 us -> none
    pallas_call x0 -> x1, Pallas kernels: none -> 83.2 us  [shards(): pl.pallas_call(kernel, out_shape=(jax.ShapeDtypeStruct((3 * ROWS, W), BF1...]
    dot_general x20 -> x0, matrix products: 56.5 us -> none  [the longest x2 11.7 us: recursion_grads(): lax.dot_general(rows_in, out_weight, (((1,), (1,)), ((), ())), preferred_...]
    another operation x13 -> x2, local copies, waits for them, and re-layouts: 50.2 us -> 3.48 us  [pair(): jnp.stack([grads[first:first + count], grads[second:second + count]], axi...]
    all_gather x2 -> x0, blocking collectives: 42 us -> none  [recursion_grads(): lax.all_gather(encode_places(places), 'seq', axis=0, tiled=True)]
    another operation x18 -> x0, other arithmetic: 25.6 us -> none  [the longest x2 24.4 us: recursion_grads(): jnp.stack([dkey.reshape(lax.axis_size('seq') * slots, HEADS * HEAD_DIM),...]
    all_to_all x4 -> x0, starting transfers between devices: 24.3 us -> none  [the longest x2 13.8 us: send_apart(): lax.all_to_all(anchor, 'seq', split_axis=0, concat_axis=0, tiled=True)]
  transfers between devices with their start and end apart: 8 -> 0, of which waited for: 4 -> 0; matrix products, arithmetic and copies ran while one was open for 9% -> 0% of each run, Pallas kernels for 0% -> 0%
where the time goes in v1:
time: 99 us; the launch traced here: 98.6 us
  Pallas kernels  83.2 us (84%)
  local copies, waits for them, and re-layouts  14.7 us (15%)
    pallas_call x1, Pallas kernels, shards(): pl.pallas_call(kernel, out_shape=(jax.ShapeDtypeStruct((3 * ROWS, W), BF1...  83.2 us
    unnamed x11, local copies, waits for them, and re-layouts  7.9 us
    another operation x2, local copies, waits for them, and re-layouts, pair(): jnp.stack([grads[first:first + count], grads[second:second + count]], axi...  3.48 us

profile of v1, /device:TPU:0, one launch (start us, length us, event | category | flops | bytes accessed | tf_op | source)
XLA Modules:
  0.0 98.6 jit_solution(17264776704886605203)
XLA Ops:
  0.6 1.3 %copy.33 = s32[2,1,256]{2,0,1:T(2,128)} copy(s32[2,1,256]{2,1,0:T(1,128)} %param.9) | data formatting | bytes 4096
  1.9 0.9 bitcast_dynamic-update-slice_fusion
  2.8 1.8 %fusion.2 = (bf16[1,48,1,2048]{3,2,1,0:T(2,128)(2,1)S(1)}, bf16[1,48,1,2048]{3,2,1,0:T(2,128)(2,1)S(1)}) fusion(bf16[1,48,2,2048]{3,2,1,0:T(2,128)(2,1)} %param.12), kind=kLoop, calls=%fused_computation.19 | loop fusion | bytes 786432 | tf_op jit(solution)/shard_map/slice | solution.py:410
  4.7 0.1 fusion.1
  4.8 0.1 fusion
  4.9 0.9 pad_dynamic-update-slice_fusion.2
  5.8 1.4 %fusion.3 = (bf16[1,24,1,2048]{3,2,1,0:T(2,128)(2,1)S(1)}, bf16[1,24,1,2048]{3,2,1,0:T(2,128)(2,1)S(1)}) fusion(bf16[1,24,2,2048]{3,2,1,0:T(2,128)(2,1)} %param.14), kind=kLoop, calls=%fused_computation.20 | loop fusion | bytes 393216 | tf_op jit(solution)/shard_map/slice | solution.py:413
  7.2 0.1 copy_bitcast_fusion.2
  7.3 0.0 copy-start
  7.4 0.9 copy-done
  8.3 83.2 %rows_attention_weight.1 = (bf16[240,2048]{1,0:T(8,128)(2,1)}, f32[16,2048]{1,0:T(8,128)}) custom-call(s32[1,256]{1,0:T(1,128)} %depths.1, s32[2,256]{1,0:T(2,128)} %bitcast.37, bf16[2,256,2048]{2,1,0:T(8,128)(2,1)} %bitcast.35, bf16[240,2048]{1,0:T(8,128)(2,1)} %copy-done, bf16[2048,2048]{1,0:T(8,128)(2,1)} %weight.1), custom_call_target="tpu_custom_call" | custom-call | flops 3000000000 | bytes 20000000 | tf_op jit(solution)/shard_map/rows_attention_weight/pallas_call | solution.py:419
  91.5 1.8 %slice_bitcast_fusion.1 = (bf16[48,1,2048]{2,0,1:T(8,128)(2,1)S(1)}, bf16[48,1,2048]{2,0,1:T(8,128)(2,1)S(1)}, bf16[1,48,2048]{2,1,0:T(8,128)(2,1)}) fusion(bf16[240,2048]{1,0:T(8,128)(2,1)} %get-tuple-element.7), kind=kLoop, calls=%fused_computation.8 | loop fusion | bytes 1179648 | tf_op jit(solution)/shard_map/stack | solution.py:465
  93.4 1.2 %copy.17 = bf16[1,48,2,2048]{3,2,1,0:T(2,128)(2,1)} copy(bf16[1,48,2,2048]{3,1,2,0:T(8,128)(2,1)S(1)} %maximum_bitcast_fusion) | data formatting | bytes 786432
  94.5 1.6 %slice_bitcast_fusion.4 = (bf16[24,1,2048]{2,0,1:T(8,128)(2,1)S(1)}, bf16[24,1,2048]{2,0,1:T(8,128)(2,1)S(1)}, bf16[1,24,2048]{2,1,0:T(8,128)(2,1)}) fusion(bf16[240,2048]{1,0:T(8,128)(2,1)} %get-tuple-element.7), kind=kLoop, calls=%fused_computation.16 | loop fusion | bytes 589824 | tf_op jit(solution)/shard_map/stack | solution.py:465
  96.2 0.9 copy.18
  97.1 1.6 %copy.40 = f32[16,2048]{1,0:T(8,128)} copy(f32[16,2048]{1,0:T(8,128)} %get-tuple-element.35) | data formatting | bytes 262144
  (4 shorter events, 0.1 us)
Async XLA Ops:
  7.3 1.0 copy-start

commit v2 on v1

--- a/solution.py
+++ b/solution.py
@@ -16,6 +16,11 @@
 NE, NL = 48, 24
 NLP = 32
 ROWS = NE + NLP
+QKV_ROWS = 3 * NE + 80
+OTHERS = (
+    (2, 2), (1, 2), (2, 1), (2, 3), (3, 2), (0, 2), (2, 0), (1, 1),
+    (3, 3), (1, 3), (3, 1), (0, 1), (1, 0), (0, 3), (3, 0),
+)
 KE, KL = N * NE, N * NL
 SCALE = E**-0.5
 
@@ -41,24 +46,44 @@
 
 
 def kernel(
-    depths, owners, cot, qkv, weight,
+    depths, owners, cot, query_early, keyval_early, query_late, keyval_late, weight,
     out, dw,
-    cotv, wv, rows_send, rows_recv, meta_send, meta_recv, qkv_recv, rows_all,
-    dout_send, dout_recv, att_send, att_recv, dqkv_send, part_send, part_recv,
+    cotv, wv, ql_v, kve_v, kvl_v, qkv_send,
+    rows_send, rows_recv, meta_send, meta_recv, qkv_recv, rows_all,
+    dout_send, dout_recv, att_send, att_recv, dqkv_send,
+    sum1_send, sum1_recv, sum2_send, sum2_recv,
     probs_e, probs_bf_e, ds_e, probs_l, probs_bf_l, ds_l,
-    local_sem, send, recv, gsend, grecv,
+    local_sem, send, recv, gsend, grecv, sum_send, sum_recv,
 ):
     d = lax.axis_index("dp")
     s = lax.axis_index("seq")
     chip = lax.div(d, 2)
     core = lax.rem(d, 2)
     partner = chip * 2 + 1 - core
-    target_dp = lax.div(s, 2)
-    parity = lax.rem(s, 2)
+    z, y = lax.div(s, 4), lax.rem(s, 4)
+
+    def head_of(j):
+        return lax.rem(chip + lax.div(j, 4) + 2 * core, 4) * 4 + lax.rem(j, 4)
+
+    def holder(of_dp, head):
+        turn = lax.div(head, 4) + 8 - lax.div(of_dp, 2) - 2 * lax.rem(of_dp, 2)
+        return lax.rem(turn, 4) * 4 + lax.rem(head, 4)
+
+    my_head = head_of(s)
+    target_dp = lax.div(my_head, 2)
+    parity = lax.rem(my_head, 2)
 
     cot_copy = pltpu.make_async_copy(cot, cotv, local_sem.at[0])
     weight_copy = pltpu.make_async_copy(weight, wv, local_sem.at[1])
+    operands = [
+        pltpu.make_async_copy(keyval_early, kve_v, local_sem.at[2]),
+        pltpu.make_async_copy(keyval_late, kvl_v, local_sem.at[3]),
+        pltpu.make_async_copy(query_early.at[0], qkv_send.at[0:NE], local_sem.at[4]),
+        pltpu.make_async_copy(query_late, ql_v, local_sem.at[5]),
+    ]
     cot_copy.start()
+    for copy in operands:
+        copy.start()
     weight_copy.start()
 
     barrier = pltpu.get_barrier_semaphore()
@@ -76,7 +101,8 @@
         greet(lax.rem(chip + i, 4) * 2 + core, s)
 
     def greet_heads(i, _):
-        from_dp, from_seq = lax.div(i, 2), 2 * d + lax.rem(i, 2)
+        from_dp = lax.div(i, 2)
+        from_seq = holder(from_dp, 2 * d + lax.rem(i, 2))
 
         @pl.when(jnp.logical_or(from_dp != d, from_seq != s))
         def _():
@@ -97,13 +123,11 @@
     below = onehot(iota((TOK, TOK), 0) < iota((TOK, TOK), 1))
     before = dot(flags, below).astype(I32)
     rank_e, rank_l = before[0:1] >> 4, before[8:9] >> 4
-    token = (iota((N, TOK), 1) + 1).astype(F32)
-    lane = iota((N, TOK), 0)
-    spread_e = jnp.where((lane == owner_e) & active_e, token, 0.0).astype(BF16)
-    spread_l = jnp.where((lane == owner_l) & active_l, token, 0.0).astype(BF16)
+    token = (iota((8, TOK), 1) + 1).astype(F32).astype(BF16)
     line = iota((E, TOK), 0)
-    meta_send[0:N] = dot_nt(spread_e, onehot(line == s * 8 + rank_e))
-    meta_send[N : 2 * N] = dot_nt(spread_l, onehot(line == s * 4 + rank_l))
+    meta_e = dot_nt(token, onehot((line == owner_e * 8 + rank_e) & active_e))
+    meta_l = dot_nt(token, onehot((line == owner_l * 4 + rank_l) & active_l))
+    meta_send[...] = jnp.where(iota((8, E), 0) < 4, meta_e, meta_l)
 
     cot_copy.wait()
     line = iota((TOK, TOK), 0)
@@ -117,6 +141,17 @@
         packed += dot(onehot(line == base + 4 * q), cotv[1, :, q * 512 : (q + 1) * 512])
     rows_send[:, :, 1024:1536] = packed.reshape(N, 16, 512).astype(BF16)
 
+    for copy in operands:
+        copy.wait()
+    qkv_send[NE : 2 * NE] = kve_v[0, :, 0, :]
+    qkv_send[2 * NE : 3 * NE] = kve_v[0, :, 1, :]
+    for c in range(4):
+        cut = slice(c * 512, (c + 1) * 512)
+        pair = kvl_v[0, :, :, cut].astype(F32)
+        qkv_send[3 * NE : QKV_ROWS, cut] = jnp.concatenate(
+            [ql_v[0, :, cut].astype(F32), pair[:, 0], pair[:, 1], jnp.zeros((8, 512), F32)], axis=0
+        ).astype(BF16)
+
     elsewhere = jnp.where(target_dp == d, 0, 1)
     pl.semaphore_wait(barrier, N - 1 + 4 + N - 1 + elsewhere)
 
@@ -130,13 +165,15 @@
             device_id_type=MESH,
         )
 
+    def other(dz, dy):
+        to_z = lax.rem(z + jnp.where(core == 0, dz, 4 - dz), 4)
+        to_y = lax.rem(y + jnp.where(core == 0, dy, 4 - dy), 4)
+        return to_z * 4 + to_y
+
     def exchange(phase, src, dst):
-        def step(i, _):
-            to = lax.rem(s + i, N)
+        for dz, dy in OTHERS:
+            to = other(dz, dy)
             remote(src(to), dst(s), phase, to, s, d).start()
-            return 0
-
-        lax.fori_loop(1, N, step, 0)
         pltpu.make_async_copy(src(s), dst(s), recv.at[phase, s]).start()
 
     def arrive(phase, src, dst):
@@ -157,25 +194,36 @@
         lax.fori_loop(1, N, step, 0)
 
     def columns(ref, j):
-        return ref.at[:, pl.ds(pl.multiple_of(j * E, E), E)]
+        return ref.at[:, pl.ds(pl.multiple_of(head_of(j) * E, E), E)]
 
     META = (0, lambda j: meta_send, lambda j: meta_recv.at[j])
     ROW = (1, lambda j: rows_send.at[j], lambda j: rows_recv.at[j])
-    QKV = (2, lambda j: columns(qkv, j), lambda j: qkv_recv.at[j])
+    QKV = (2, lambda j: columns(qkv_send, j), lambda j: qkv_recv.at[j])
     DOUT = (3, lambda j: columns(dout_send, j), lambda j: dout_recv.at[j])
     GRAD = (4, lambda j: dqkv_send.at[j], lambda j: columns(out, j))
-    PART = (5, lambda j: part_send.at[j], lambda j: part_recv.at[j])
 
     exchange(*META)
     exchange(*ROW)
     exchange(*QKV)
 
     arrive(*META)
-    token_e = jnp.zeros((N, E), F32)
-    token_l = jnp.zeros((N, E), F32)
-    for j in range(N):
-        token_e += meta_recv[j, 0:N]
-        token_l += meta_recv[j, N : 2 * N]
+
+    def spread(first, shift):
+        lane = iota((N, E), 1)
+        mine = (lane >> shift) == iota((N, E), 0)
+        wide = jnp.concatenate(
+            [jnp.where(mine, meta_recv[j, first : first + 1], 0.0) for j in range(N)], axis=0
+        )
+        low = (1 << shift) - 1
+        same = onehot((iota((E, E), 0) & low) == (iota((E, E), 1) & low))
+        wide = dot(wide.astype(BF16), same)
+        total = jnp.zeros((N, E), F32)
+        for j in range(N):
+            total += jnp.where((lane >> shift) == j, wide[j * N : (j + 1) * N], 0.0)
+        return total
+
+    token_e = spread(0, 3)
+    token_l = spread(4, 2)
 
     def tables(token, shift, slots, padded):
         peak = 1 << shift
@@ -247,9 +295,8 @@
 
     arrive(*QKV)
 
-    def late(ref, first):
-        wide = ref[:, first : first + NLP, :].astype(F32)[:, 0:NL, :]
-        return wide.reshape(KL, E)
+    def late(wide, part):
+        return wide[:, part * NL : (part + 1) * NL].reshape(KL, E)
 
     def softmax(query, key, value, row, col):
         scores = dot_nt(query, key) * SCALE
@@ -269,9 +316,8 @@
         probs_e[b * 192 : (b + 1) * 192] = probs
         probs_bf_e[b * 192 : (b + 1) * 192] = probs_bf
         att_send[4 * b : 4 * b + 4, 0:NE, :] = attended.reshape(4, NE, E).astype(BF16)
-    query_l = late(qkv_recv, 144).astype(BF16)
-    key_l = late(qkv_recv, 176).astype(BF16)
-    value_l = late(qkv_recv, 208).astype(BF16)
+    wide = qkv_recv[:, 3 * NE : QKV_ROWS, :].astype(F32)
+    query_l, key_l, value_l = (late(wide, part).astype(BF16) for part in range(3))
     gap = jnp.zeros((8, NLP - NL, E), F32)
     for b in range(2):
         query = query_l[b * 192 : (b + 1) * 192]
@@ -282,7 +328,7 @@
         attended = jnp.concatenate([attended.reshape(8, NL, E), gap], axis=1)
         att_send[8 * b : 8 * b + 8, NE:ROWS, :] = attended.astype(BF16)
 
-    ATT = 6
+    ATT = 5
 
     def att_copy(to):
         return remote(att_send.at[to], att_recv.at[d, parity], ATT, to, d * 2 + parity, target_dp)
@@ -292,11 +338,8 @@
             att_send.at[s], att_recv.at[d, parity], recv.at[ATT, d * 2 + parity]
         )
 
-    def att_step(i, _):
-        att_copy(lax.rem(s + i, N)).start()
-        return 0
-
-    lax.fori_loop(1, N, att_step, 0)
+    for dz, dy in OTHERS:
+        att_copy(other(dz, dy)).start()
 
     @pl.when(target_dp == d)
     def _():
@@ -305,10 +348,6 @@
     @pl.when(target_dp != d)
     def _():
         att_copy(s).start()
-
-    for i in (1, 3, 2):
-        gather(same_core(i), i, partner).wait_recv()
-        gather(same_core(i), 3 + i, partner).start()
 
     arrive(*DOUT)
 
@@ -327,16 +366,16 @@
         )
         ds_e[b * 192 : (b + 1) * 192] = dscores
         dqkv_send[4 * b : 4 * b + 4, 0:NE, :] = dquery.reshape(4, NE, E).astype(BF16)
-    dout_l = late(dout_recv, NE).astype(BF16)
-    attended_l = late(att_send, NE)
+    dout_l = late(dout_recv[:, NE:ROWS, :].astype(F32), 0).astype(BF16)
+    attended_l = late(att_send[:, NE:ROWS, :].astype(F32), 0)
+    dquery_l = []
     for b in range(2):
         dscores, dquery = backward(
             None, key_l, value_l, dout_l[b * 192 : (b + 1) * 192],
             attended_l[b * 192 : (b + 1) * 192], probs_l[b * 192 : (b + 1) * 192]
         )
         ds_l[b * 192 : (b + 1) * 192] = dscores
-        dquery = jnp.concatenate([dquery.reshape(8, NL, E), gap], axis=1)
-        dqkv_send[8 * b : 8 * b + 8, 144:176, :] = dquery.astype(BF16)
+        dquery_l.append(dquery)
     query_e = qkv_recv[:, 0:NE, :].reshape(KE, E)
     dout_e = dout_recv[:, 0:NE, :].reshape(KE, E)
     for c in range(2):
@@ -344,14 +383,17 @@
         dqkv_send[8 * c : 8 * c + 8, NE : 2 * NE, :] = dkey.reshape(8, NE, E).astype(BF16)
         dvalue = dot_tn(probs_bf_e[:, c * 384 : (c + 1) * 384], dout_e)
         dqkv_send[8 * c : 8 * c + 8, 2 * NE : 3 * NE, :] = dvalue.reshape(8, NE, E).astype(BF16)
-    gap = jnp.zeros((N, NLP - NL, E), F32)
+    dquery = jnp.concatenate(dquery_l, axis=0)
     dkey = dot_tn(ds_l[...], query_l) * SCALE
-    dkey = jnp.concatenate([dkey.reshape(N, NL, E), gap], axis=1)
-    dqkv_send[:, 176:208, :] = dkey.astype(BF16)
     dvalue = dot_tn(probs_bf_l[...], dout_l)
-    dvalue = jnp.concatenate([dvalue.reshape(N, NL, E), gap], axis=1)
-    dqkv_send[:, 208:240, :] = dvalue.astype(BF16)
+    parts = [part.reshape(N, NL, E) for part in (dquery, dkey, dvalue)]
+    parts.append(jnp.zeros((N, 8, E), F32))
+    dqkv_send[:, 3 * NE : QKV_ROWS, :] = jnp.concatenate(parts, axis=1).astype(BF16)
     exchange(*GRAD)
+
+    for i in (1, 3, 2):
+        gather(same_core(i), i, partner).wait_recv()
+        gather(same_core(i), 3 + i, partner).start()
 
     def att_wait(i, _):
         sender = lax.div(i, 2)
@@ -368,19 +410,57 @@
     for p in range(2):
         attended = att_recv[:, p].reshape(DP * ROWS, E)
         for c in range(4):
+            half, cut = c // 2, slice((c % 2) * 512, (c % 2) * 512 + 512)
             part = dot_tn(attended, rows[:, c * 512 : (c + 1) * 512])
-            part_send[8 * p : 8 * p + 8, :, c * 512 : (c + 1) * 512] = part.reshape(
-                8, 16, 512
-            ).astype(BF16)
-    exchange(*PART)
-    arrive(*PART)
-    total = part_recv[0].astype(F32)
-    for j in range(1, N):
-        total += part_recv[j].astype(F32)
-    dw[...] = total
+            part = part.reshape(2, 4, 16, 512).astype(BF16)
+            if half == 0:
+                sum1_send[0, 2 * p : 2 * p + 2, :, :, cut] = part
+            else:
+                for i in range(2):
+                    for j in range(4):
+                        sum1_send[1, j, 2 * p + i, :, cut] = part[i, j]
+
+    def along(half, stage, i):
+        if half == stage:
+            to = lax.rem(z + i, 4)
+            return to, to * 4 + y
+        to = lax.rem(y + i, 4)
+        return to, z * 4 + to
+
+    def sum_copy(half, stage, i):
+        source, target = (sum1_send, sum1_recv) if stage == 0 else (sum2_send, sum2_recv)
+        to, device = along(half, stage, i)
+        return pltpu.make_async_remote_copy(
+            src_ref=source.at[half, to],
+            dst_ref=target.at[half, i - 1],
+            send_sem=sum_send.at[stage, half, i - 1],
+            recv_sem=sum_recv.at[stage, half, i - 1],
+            device_id=(d, device),
+            device_id_type=MESH,
+        )
+
+    for i in (2, 1, 3):
+        for half in range(2):
+            sum_copy(half, 0, i).start()
+    for half in range(2):
+        for i in range(1, 4):
+            sum_copy(half, 0, i).wait_recv()
+        total = sum1_send[half, z if half == 0 else y].astype(F32)
+        for i in range(3):
+            total += sum1_recv[half, i].astype(F32)
+        sum2_send[half] = total.astype(BF16)
+        for i in (2, 1, 3):
+            sum_copy(half, 1, i).start()
+    for half in range(2):
+        for i in range(1, 4):
+            sum_copy(half, 1, i).wait_recv()
+        total = sum2_send[half, y if half == 0 else z].astype(F32)
+        for i in range(3):
+            total += sum2_recv[half, i].astype(F32)
+        dw[:, half * 1024 : (half + 1) * 1024] = total
     arrive(*GRAD)
 
-    for phase in (META, ROW, QKV, DOUT, GRAD, PART):
+    for phase in (META, ROW, QKV, DOUT, GRAD):
         sent(*phase)
 
     def att_sent(i, _):
@@ -395,62 +475,71 @@
 
     for i in range(7):
         gather(d, i, partner).wait_send()
+    for stage in range(2):
+        for half in range(2):
+            for i in range(1, 4):
+                sum_copy(half, stage, i).wait_send()
+
+
+def finish(grads, dw, dquery_early, dkeyval_early, dquery_late, dkeyval_late, dweight):
+    dquery_early[0] = grads[0:NE]
+    dkeyval_early[0] = jnp.stack([grads[NE : 2 * NE], grads[2 * NE : 3 * NE]], axis=1)
+    late = grads[3 * NE : QKV_ROWS].astype(F32)
+    dquery_late[0] = late[0:NL].astype(BF16)
+    dkeyval_late[0] = jnp.stack(
+        [late[NL : 2 * NL].astype(BF16), late[2 * NL : 3 * NL].astype(BF16)], axis=1
+    )
+    dweight[...] = dw[...]
 
 
 def shards(
     depths, owners, cotangent, query_early, keyval_early, query_late, keyval_late, out_weight
 ):
-    def late(rows):
-        return jnp.pad(rows, ((0, NLP - NL), (0, 0)))
-
-    qkv = jnp.concatenate(
-        [
-            query_early[0],
-            keyval_early[0, :, 0],
-            keyval_early[0, :, 1],
-            late(query_late[0]),
-            late(keyval_late[0, :, 0]),
-            late(keyval_late[0, :, 1]),
-        ],
-        axis=0,
-    )
     vmem = pl.BlockSpec(memory_space=pltpu.VMEM)
     hbm = pl.BlockSpec(memory_space=pl.ANY)
-    grads, dweight = pl.pallas_call(
+    grads, dw = pl.pallas_call(
         kernel,
         out_shape=(
-            jax.ShapeDtypeStruct((3 * ROWS, W), BF16),
+            jax.ShapeDtypeStruct((QKV_ROWS, W), BF16),
             jax.ShapeDtypeStruct((N, W), F32),
         ),
-        in_specs=[vmem, vmem, hbm, hbm, hbm],
+        in_specs=[vmem, vmem] + [hbm] * 6,
         out_specs=(hbm, vmem),
         scratch_shapes=[
             pltpu.VMEM((2, TOK, W), BF16),
             pltpu.VMEM((W, W), BF16),
+            pltpu.VMEM((1, NL, W), BF16),
+            pltpu.VMEM((1, NE, 2, W), BF16),
+            pltpu.VMEM((1, NL, 2, W), BF16),
+            pltpu.VMEM((QKV_ROWS, W), BF16),
             pltpu.VMEM((N, 16, 1536), BF16),
             pltpu.VMEM((N, 16, 1536), BF16),
-            pltpu.VMEM((2 * N, E), F32),
-            pltpu.VMEM((N, 2 * N, E), F32),
-            pltpu.VMEM((N, 3 * ROWS, E), BF16),
+            pltpu.VMEM((8, E), F32),
+            pltpu.VMEM((N, 8, E), F32),
+            pltpu.VMEM((N, QKV_ROWS, E), BF16),
             pltpu.VMEM((DP, ROWS, W), BF16),
             pltpu.VMEM((ROWS, W), BF16),
             pltpu.VMEM((N, ROWS, E), BF16),
             pltpu.VMEM((N, ROWS, E), BF16),
             pltpu.VMEM((DP, 2, ROWS, E), BF16),
-            pltpu.VMEM((N, 3 * ROWS, E), BF16),
-            pltpu.VMEM((N, N, W), BF16),
-            pltpu.VMEM((N, N, W), BF16),
+            pltpu.VMEM((N, QKV_ROWS, E), BF16),
+            pltpu.VMEM((2, 4, 4, 16, W // 2), BF16),
+            pltpu.VMEM((2, 3, 4, 16, W // 2), BF16),
+            pltpu.VMEM((2, 4, 16, W // 2), BF16),
+            pltpu.VMEM((2, 3, 16, W // 2), BF16),
             pltpu.VMEM((KE, KE), F32),
             pltpu.VMEM((KE, KE), BF16),
             pltpu.VMEM((KE, KE), BF16),
             pltpu.VMEM((KL, KL), F32),
             pltpu.VMEM((KL, KL), BF16),
             pltpu.VMEM((KL, KL), BF16),
-            pltpu.SemaphoreType.DMA((2,)),
-            pltpu.SemaphoreType.DMA((7, N)),
-            pltpu.SemaphoreType.DMA((7, N)),
+            pltpu.SemaphoreType.DMA((6,)),
+            pltpu.SemaphoreType.DMA((6, N)),
+            pltpu.SemaphoreType.DMA((6, N)),
             pltpu.SemaphoreType.DMA((7,)),
             pltpu.SemaphoreType.DMA((DP,)),
+            pltpu.SemaphoreType.DMA((2, 2, 3)),
+            pltpu.SemaphoreType.DMA((2, 2, 3)),
         ],
         compiler_params=pltpu.CompilerParams(
             collective_id=0, has_side_effects=True, vmem_limit_bytes=56 * 1024 * 1024
@@ -459,20 +548,24 @@
             flops=3_000_000_000, bytes_accessed=20_000_000, transcendentals=800_000
         ),
         name="rows_attention_weight",
-    )(depths, owners[:, 0], cotangent[:, 0], qkv, out_weight)
-
-    def pair(first, second, count):
-        return jnp.stack(
-            [grads[first : first + count], grads[second : second + count]], axis=1
-        )[None]
-
-    return (
-        grads[None, 0:NE],
-        pair(NE, 2 * NE, NE),
-        grads[None, 144 : 144 + NL],
-        pair(176, 208, NL),
-        dweight,
+    )(
+        depths, owners, cotangent[:, 0], query_early, keyval_early, query_late, keyval_late,
+        out_weight,
     )
+    return pl.pallas_call(
+        finish,
+        out_shape=(
+            jax.ShapeDtypeStruct(query_early.shape, BF16),
+            jax.ShapeDtypeStruct(keyval_early.shape, BF16),
+            jax.ShapeDtypeStruct(query_late.shape, BF16),
+            jax.ShapeDtypeStruct(keyval_late.shape, BF16),
+            jax.ShapeDtypeStruct((N, W), F32),
+        ),
+        in_specs=[vmem] * 2,
+        out_specs=(vmem,) * 5,
+        compiler_params=pltpu.CompilerParams(vmem_limit_bytes=32 * 1024 * 1024),
+        name="outputs",
+    )(grads, dw)
 
 
 def solution(mesh):

time: 99 us -> 71.2 us (0.72)
  Pallas kernels: 83.2 us -> 68 us
  local copies, waits for them, and re-layouts: 14.7 us -> 2.08 us
    pallas_call x1 -> x2, Pallas kernels: 83.2 us -> 68 us  [the longest x1 66.3 us: shards(): pl.pallas_call(kernel, out_shape=(jax.ShapeDtypeStruct((QKV_ROWS, W), BF1...]
    unnamed x11 -> x4, local copies, waits for them, and re-layouts: 7.9 us -> 2.08 us
    another operation x2 -> x0, local copies, waits for them, and re-layouts: 3.48 us -> none  [pair(): jnp.stack([grads[first:first + count], grads[second:second + count]], axi...]
    slice x2 -> x0, local copies, waits for them, and re-layouts: 3.18 us -> none  [the longest x1 1.82 us: shards(): keyval_early[0, :, 1]]
where the time goes in v2:
time: 71.2 us; the launch traced here: 70.7 us
  Pallas kernels  68 us (96%)
  local copies, waits for them, and re-layouts  2.08 us (3%)
    pallas_call x1, Pallas kernels, shards(): pl.pallas_call(kernel, out_shape=(jax.ShapeDtypeStruct((QKV_ROWS, W), BF1...  66.3 us
    unnamed x4, local copies, waits for them, and re-layouts  2.08 us
    pallas_call x1, Pallas kernels, shards(): pl.pallas_call(finish, out_shape=(jax.ShapeDtypeStruct(query_early.shape,...  1.74 us

profile of v2, /device:TPU:0, one launch (start us, length us, event | category | flops | bytes accessed | tf_op | source)
XLA Modules:
  0.0 70.7 jit_solution(14942833162921803482)
XLA Ops:
  0.6 66.3 %rows_attention_weight.1 = (bf16[224,2048]{1,0:T(8,128)(2,1)}, f32[16,2048]{1,0:T(8,128)}) custom-call(s32[1,256]{1,0:T(1,128)} %depths.1, s32[2,1,256]{2,1,0:T(1,128)} %owners.1, bf16[2,256,2048]{2,1,0:T(8,128)(2,1)} %bitcast.1, bf16[1,48,2048]{2,1,0:T(8,128)(2,1)} %query_early.1, bf16[1,48,2,2048]{3,2,1,0:T(2,128)(2,1)} %keyval_early.1, ...), custom_call_target="tpu_custom_call" | custom-call | flops 3000000000 | bytes 20000000 | tf_op jit(solution)/shard_map/rows_attention_weight/pallas_call | solution.py:500
  66.9 0.0 copy-start
  66.9 1.2 %copy-done = bf16[224,2048]{1,0:T(8,128)(2,1)S(1)} copy-done((bf16[224,2048]{1,0:T(8,128)(2,1)S(1)}, bf16[224,2048]{1,0:T(8,128)(2,1)}, u32[]{:S(2)}) %copy-start) | copy-done | bytes 917528
  68.1 0.0 copy-start.1
  68.1 0.9 %copy-done.1 = f32[16,2048]{1,0:T(8,128)S(1)} copy-done((f32[16,2048]{1,0:T(8,128)S(1)}, f32[16,2048]{1,0:T(8,128)}, u32[]{:S(2)}) %copy-start.1) | copy-done | bytes 131096
  69.0 1.7 %outputs.1 = (bf16[1,48,2048]{2,1,0:T(8,128)(2,1)}, bf16[1,48,2,2048]{3,2,1,0:T(2,128)(2,1)}, bf16[1,24,2048]{2,1,0:T(8,128)(2,1)}, bf16[1,24,2,2048]{3,2,1,0:T(2,128)(2,1)}, f32[16,2048]{1,0:T(8,128)}) custom-call(bf16[224,2048]{1,0:T(8,128)(2,1)S(1)} %copy-done, f32[16,2048]{1,0:T(8,128)S(1)} %copy-done.1), custom_call_target="tpu_custom_call" | custom-call | tf_op jit(solution)/shard_map/outputs/pallas_call | solution.py:555
Async XLA Ops:
  66.9 1.2 %copy-start = (bf16[224,2048]{1,0:T(8,128)(2,1)S(1)}, bf16[224,2048]{1,0:T(8,128)(2,1)}, u32[]{:S(2)}) copy-start(bf16[224,2048]{1,0:T(8,128)(2,1)} %get-tuple-element.7.grads) | copy-start | bytes 2752516
  68.1 0.9 %copy-start.1 = (f32[16,2048]{1,0:T(8,128)S(1)}, f32[16,2048]{1,0:T(8,128)}, u32[]{:S(2)}) copy-start(f32[16,2048]{1,0:T(8,128)} %get-tuple-element.8.dw) | copy-start | bytes 393220

commit v3 on v2

--- a/solution.py
+++ b/solution.py
@@ -48,10 +48,11 @@
 def kernel(
     depths, owners, cot, query_early, keyval_early, query_late, keyval_late, weight,
     out, dw,
-    cotv, wv, ql_v, kve_v, kvl_v, qkv_send,
+    depth_v, owner_v, cotv, wv, ql_v, kve_v, kvl_v, qkv_send,
     rows_send, rows_recv, meta_send, meta_recv, qkv_recv, rows_all,
     dout_send, dout_recv, att_send, att_recv, dqkv_send,
     sum1_send, sum1_recv, sum2_send, sum2_recv,
+    dw_v,
     probs_e, probs_bf_e, ds_e, probs_l, probs_bf_l, ds_l,
     local_sem, send, recv, gsend, grecv, sum_send, sum_recv,
 ):
@@ -69,21 +70,28 @@
         turn = lax.div(head, 4) + 8 - lax.div(of_dp, 2) - 2 * lax.rem(of_dp, 2)
         return lax.rem(turn, 4) * 4 + lax.rem(head, 4)
 
+    def same_core(i):
+        return lax.rem(chip + i, 4) * 2 + core
+
     my_head = head_of(s)
     target_dp = lax.div(my_head, 2)
     parity = lax.rem(my_head, 2)
 
     cot_copy = pltpu.make_async_copy(cot, cotv, local_sem.at[0])
     weight_copy = pltpu.make_async_copy(weight, wv, local_sem.at[1])
+    routing = [
+        pltpu.make_async_copy(depths, depth_v, local_sem.at[6]),
+        pltpu.make_async_copy(owners, owner_v, local_sem.at[7]),
+    ]
     operands = [
         pltpu.make_async_copy(keyval_early, kve_v, local_sem.at[2]),
+        pltpu.make_async_copy(query_late, ql_v, local_sem.at[5]),
         pltpu.make_async_copy(keyval_late, kvl_v, local_sem.at[3]),
         pltpu.make_async_copy(query_early.at[0], qkv_send.at[0:NE], local_sem.at[4]),
-        pltpu.make_async_copy(query_late, ql_v, local_sem.at[5]),
     ]
+    for copy in routing + operands:
+        copy.start()
     cot_copy.start()
-    for copy in operands:
-        copy.start()
     weight_copy.start()
 
     barrier = pltpu.get_barrier_semaphore()
@@ -97,8 +105,8 @@
 
     lax.fori_loop(1, N, greet_seq, 0)
     greet(partner, s)
-    for i in range(1, 4):
-        greet(lax.rem(chip + i, 4) * 2 + core, s)
+    for i in (1, 3):
+        greet(same_core(i), s)
 
     def greet_heads(i, _):
         from_dp = lax.div(i, 2)
@@ -112,9 +120,11 @@
 
     lax.fori_loop(0, 2 * DP, greet_heads, 0)
 
-    depth = depths[...]
+    for copy in routing:
+        copy.wait()
+    depth = depth_v[...]
     active_e, active_l = depth > 1, depth > 2
-    owner_e, owner_l = owners[0], owners[1]
+    owner_e, owner_l = owner_v[0], owner_v[1]
     flags = jnp.where(
         iota((16, TOK), 0) < 8,
         jnp.broadcast_to(active_e.astype(F32), (16, TOK)),
@@ -129,6 +139,17 @@
     meta_l = dot_nt(token, onehot((line == owner_l * 4 + rank_l) & active_l))
     meta_send[...] = jnp.where(iota((8, E), 0) < 4, meta_e, meta_l)
 
+    for copy in operands:
+        copy.wait()
+    qkv_send[NE : 2 * NE] = kve_v[0, :, 0, :]
+    qkv_send[2 * NE : 3 * NE] = kve_v[0, :, 1, :]
+    for c in range(4):
+        cut = slice(c * 512, (c + 1) * 512)
+        pair = kvl_v[0, :, :, cut].astype(F32)
+        qkv_send[3 * NE : QKV_ROWS, cut] = jnp.concatenate(
+            [ql_v[0, :, cut].astype(F32), pair[:, 0], pair[:, 1], jnp.zeros((8, 512), F32)], axis=0
+        ).astype(BF16)
+
     cot_copy.wait()
     line = iota((TOK, TOK), 0)
     base = jnp.where(active_e, owner_e * 16 + rank_e, -64)
@@ -141,66 +162,55 @@
         packed += dot(onehot(line == base + 4 * q), cotv[1, :, q * 512 : (q + 1) * 512])
     rows_send[:, :, 1024:1536] = packed.reshape(N, 16, 512).astype(BF16)
 
-    for copy in operands:
-        copy.wait()
-    qkv_send[NE : 2 * NE] = kve_v[0, :, 0, :]
-    qkv_send[2 * NE : 3 * NE] = kve_v[0, :, 1, :]
-    for c in range(4):
-        cut = slice(c * 512, (c + 1) * 512)
-        pair = kvl_v[0, :, :, cut].astype(F32)
-        qkv_send[3 * NE : QKV_ROWS, cut] = jnp.concatenate(
-            [ql_v[0, :, cut].astype(F32), pair[:, 0], pair[:, 1], jnp.zeros((8, 512), F32)], axis=0
-        ).astype(BF16)
-
     elsewhere = jnp.where(target_dp == d, 0, 1)
-    pl.semaphore_wait(barrier, N - 1 + 4 + N - 1 + elsewhere)
-
-    def remote(src, dst, phase, to, sender, to_dp):
+    pl.semaphore_wait(barrier, N - 1 + 3 + N - 1 + elsewhere)
+
+    def remote(src, dst, phase, to, to_dp):
         return pltpu.make_async_remote_copy(
             src_ref=src,
             dst_ref=dst,
-            send_sem=send.at[phase, to],
-            recv_sem=recv.at[phase, sender],
+            send_sem=send.at[phase],
+            recv_sem=recv.at[phase],
             device_id=(to_dp, to),
             device_id_type=MESH,
         )
+
+    def wait_bytes(ref, sem):
+        pltpu.make_async_copy(ref, ref, sem).wait()
 
     def other(dz, dy):
         to_z = lax.rem(z + jnp.where(core == 0, dz, 4 - dz), 4)
         to_y = lax.rem(y + jnp.where(core == 0, dy, 4 - dy), 4)
         return to_z * 4 + to_y
 
-    def exchange(phase, src, dst):
+    def exchange(phase, src, dst, whole):
         for dz, dy in OTHERS:
             to = other(dz, dy)
-            remote(src(to), dst(s), phase, to, s, d).start()
-        pltpu.make_async_copy(src(s), dst(s), recv.at[phase, s]).start()
-
-    def arrive(phase, src, dst):
-        def step(i, _):
-            sender = lax.rem(s + i, N)
-            remote(src(sender), dst(sender), phase, sender, sender, d).wait_recv()
-            return 0
-
-        lax.fori_loop(1, N, step, 0)
-        pltpu.make_async_copy(src(s), dst(s), recv.at[phase, s]).wait()
-
-    def sent(phase, src, dst):
-        def step(i, _):
-            to = lax.rem(s + i, N)
-            remote(src(to), dst(s), phase, to, s, d).wait_send()
-            return 0
-
-        lax.fori_loop(1, N, step, 0)
+            remote(src(to), dst(s), phase, to, d).start()
+        pltpu.make_async_copy(src(s), dst(s), recv.at[phase]).start()
+
+    def arrive(phase, src, dst, whole):
+        wait_bytes(whole, recv.at[phase])
 
     def columns(ref, j):
         return ref.at[:, pl.ds(pl.multiple_of(head_of(j) * E, E), E)]
 
-    META = (0, lambda j: meta_send, lambda j: meta_recv.at[j])
-    ROW = (1, lambda j: rows_send.at[j], lambda j: rows_recv.at[j])
-    QKV = (2, lambda j: columns(qkv_send, j), lambda j: qkv_recv.at[j])
-    DOUT = (3, lambda j: columns(dout_send, j), lambda j: dout_recv.at[j])
-    GRAD = (4, lambda j: dqkv_send.at[j], lambda j: columns(out, j))
+    META = (0, lambda j: meta_send, lambda j: meta_recv.at[j], meta_recv)
+    ROW = (1, lambda j: rows_send.at[j], lambda j: rows_recv.at[j], rows_recv)
+    QKV = (2, lambda j: columns(qkv_send, j), lambda j: qkv_recv.at[j], qkv_recv)
+    DOUT = (3, lambda j: columns(dout_send, j), lambda j: dout_recv.at[j], dout_recv)
+
+    def grads(phase, first, last):
+        return (
+            phase,
+            lambda j: dqkv_send.at[j, first:last],
+            lambda j: columns(out.at[first:last], j),
+            out.at[first:last],
+        )
+
+    GRAD_Q, GRAD_LATE = grads(4, 0, NE), grads(5, 3 * NE, QKV_ROWS)
+    GRAD_KV = grads(6, NE, 3 * NE)
+    ATT = 7
 
     exchange(*META)
     exchange(*ROW)
@@ -269,22 +279,36 @@
         got = dot(pick, rows_recv[:, :, 1024:1536].reshape(TOK, 512))
         rows_all[d, NE:ROWS, q * 512 : (q + 1) * 512] = got.astype(BF16)
 
-    def gather(block, index, to_dp):
+    def gather(block, kind, to_dp, half=None):
+        part = rows_all.at[block]
+        if half is not None:
+            part = part.at[:, half * 1024 : (half + 1) * 1024]
         return pltpu.make_async_remote_copy(
-            src_ref=rows_all.at[block],
-            dst_ref=rows_all.at[block],
-            send_sem=gsend.at[index],
-            recv_sem=grecv.at[block],
+            src_ref=part,
+            dst_ref=part,
+            send_sem=gsend,
+            recv_sem=grecv.at[kind],
             device_id=(to_dp, s),
             device_id_type=MESH,
         )
 
-    def same_core(i):
-        return lax.rem(chip + i, 4) * 2 + core
-
-    gather(d, 0, partner).start()
-    for i in (2, 1, 3):
-        gather(d, i, same_core(i)).start()
+    ahead, behind, far = same_core(1), same_core(3), same_core(2)
+    FROM_BEHIND, FROM_AHEAD, FROM_FAR, FROM_PARTNER = range(4)
+    gather(d, FROM_BEHIND, ahead).start()
+    gather(d, FROM_AHEAD, behind).start()
+    gather(d, FROM_PARTNER, partner).start()
+
+    def gather_near():
+        wait_bytes(rows_all.at[behind], grecv.at[FROM_BEHIND])
+        gather(behind, FROM_FAR, ahead, 1).start()
+        gather(behind, FROM_PARTNER, partner).start()
+        wait_bytes(rows_all.at[ahead], grecv.at[FROM_AHEAD])
+        gather(ahead, FROM_FAR, behind, 0).start()
+        gather(ahead, FROM_PARTNER, partner).start()
+
+    def gather_far():
+        wait_bytes(rows_all.at[far], grecv.at[FROM_FAR])
+        gather(far, FROM_PARTNER, partner).start()
 
     weight_copy.wait()
     mine = rows_all[d]
@@ -294,6 +318,7 @@
     exchange(*DOUT)
 
     arrive(*QKV)
+    gather_near()
 
     def late(wide, part):
         return wide[:, part * NL : (part + 1) * NL].reshape(KL, E)
@@ -306,6 +331,25 @@
         probs = weights / jnp.sum(weights, axis=1, keepdims=True)
         probs_bf = probs.astype(BF16)
         return probs, probs_bf, dot(probs_bf, value)
+
+    def attended_out(first, last):
+        def copy(to):
+            return remote(
+                att_send.at[to, first:last], att_recv.at[d, parity, first:last], ATT, to, target_dp
+            )
+
+        for dz, dy in OTHERS:
+            copy(other(dz, dy)).start()
+
+        @pl.when(target_dp == d)
+        def _():
+            pltpu.make_async_copy(
+                att_send.at[s, first:last], att_recv.at[d, parity, first:last], recv.at[ATT]
+            ).start()
+
+        @pl.when(target_dp != d)
+        def _():
+            copy(s).start()
 
     key_e = qkv_recv[:, NE : 2 * NE, :].reshape(KE, E)
     value_e = qkv_recv[:, 2 * NE : 3 * NE, :].reshape(KE, E)
@@ -316,6 +360,7 @@
         probs_e[b * 192 : (b + 1) * 192] = probs
         probs_bf_e[b * 192 : (b + 1) * 192] = probs_bf
         att_send[4 * b : 4 * b + 4, 0:NE, :] = attended.reshape(4, NE, E).astype(BF16)
+    attended_out(0, NE)
     wide = qkv_recv[:, 3 * NE : QKV_ROWS, :].astype(F32)
     query_l, key_l, value_l = (late(wide, part).astype(BF16) for part in range(3))
     gap = jnp.zeros((8, NLP - NL, E), F32)
@@ -327,27 +372,7 @@
         probs_bf_l[b * 192 : (b + 1) * 192] = probs_bf
         attended = jnp.concatenate([attended.reshape(8, NL, E), gap], axis=1)
         att_send[8 * b : 8 * b + 8, NE:ROWS, :] = attended.astype(BF16)
-
-    ATT = 5
-
-    def att_copy(to):
-        return remote(att_send.at[to], att_recv.at[d, parity], ATT, to, d * 2 + parity, target_dp)
-
-    def att_local():
-        return pltpu.make_async_copy(
-            att_send.at[s], att_recv.at[d, parity], recv.at[ATT, d * 2 + parity]
-        )
-
-    for dz, dy in OTHERS:
-        att_copy(other(dz, dy)).start()
-
-    @pl.when(target_dp == d)
-    def _():
-        att_local().start()
-
-    @pl.when(target_dp != d)
-    def _():
-        att_copy(s).start()
+    attended_out(NE, ROWS)
 
     arrive(*DOUT)
 
@@ -366,6 +391,7 @@
         )
         ds_e[b * 192 : (b + 1) * 192] = dscores
         dqkv_send[4 * b : 4 * b + 4, 0:NE, :] = dquery.reshape(4, NE, E).astype(BF16)
+    exchange(*GRAD_Q)
     dout_l = late(dout_recv[:, NE:ROWS, :].astype(F32), 0).astype(BF16)
     attended_l = late(att_send[:, NE:ROWS, :].astype(F32), 0)
     dquery_l = []
@@ -389,23 +415,11 @@
     parts = [part.reshape(N, NL, E) for part in (dquery, dkey, dvalue)]
     parts.append(jnp.zeros((N, 8, E), F32))
     dqkv_send[:, 3 * NE : QKV_ROWS, :] = jnp.concatenate(parts, axis=1).astype(BF16)
-    exchange(*GRAD)
-
-    for i in (1, 3, 2):
-        gather(same_core(i), i, partner).wait_recv()
-        gather(same_core(i), 3 + i, partner).start()
-
-    def att_wait(i, _):
-        sender = lax.div(i, 2)
-        remote(
-            att_send.at[0], att_recv.at[sender, lax.rem(i, 2)], ATT, s, i, target_dp
-        ).wait_recv()
-        return 0
-
-    lax.fori_loop(0, 2 * DP, att_wait, 0)
-    gather(partner, 0, partner).wait_recv()
-    for i in (1, 3, 2):
-        gather(lax.rem(chip + i, 4) * 2 + 1 - core, i, partner).wait_recv()
+    exchange(*GRAD_LATE)
+    gather_far()
+
+    wait_bytes(att_recv, recv.at[ATT])
+    wait_bytes(rows_all.at[0:4], grecv.at[FROM_PARTNER])
     rows = rows_all[...].reshape(DP * ROWS, W)
     for p in range(2):
         attended = att_recv[:, p].reshape(DP * ROWS, E)
@@ -433,8 +447,8 @@
         return pltpu.make_async_remote_copy(
             src_ref=source.at[half, to],
             dst_ref=target.at[half, i - 1],
-            send_sem=sum_send.at[stage, half, i - 1],
-            recv_sem=sum_recv.at[stage, half, i - 1],
+            send_sem=sum_send.at[stage],
+            recv_sem=sum_recv.at[stage, half],
             device_id=(d, device),
             device_id_type=MESH,
         )
@@ -442,70 +456,112 @@
     for i in (2, 1, 3):
         for half in range(2):
             sum_copy(half, 0, i).start()
+    exchange(*GRAD_KV)
     for half in range(2):
-        for i in range(1, 4):
-            sum_copy(half, 0, i).wait_recv()
+        wait_bytes(sum1_recv.at[half], sum_recv.at[0, half])
         total = sum1_send[half, z if half == 0 else y].astype(F32)
         for i in range(3):
             total += sum1_recv[half, i].astype(F32)
         sum2_send[half] = total.astype(BF16)
         for i in (2, 1, 3):
             sum_copy(half, 1, i).start()
+
+    wait_bytes(meta_recv.at[1:N], send.at[META[0]])
+    wait_bytes(rows_recv.at[1:N], send.at[ROW[0]])
+    wait_bytes(qkv_recv.at[1:N], send.at[QKV[0]])
+    wait_bytes(dout_recv.at[1:N], send.at[DOUT[0]])
+
+    @pl.when(target_dp == d)
+    def _():
+        wait_bytes(att_send.at[1:N], send.at[ATT])
+
+    @pl.when(target_dp != d)
+    def _():
+        wait_bytes(att_send, send.at[ATT])
+
+    wait_bytes(rows_all.at[1:DP], gsend)
+    wait_bytes(sum1_recv, sum_send.at[0])
+
     for half in range(2):
-        for i in range(1, 4):
-            sum_copy(half, 1, i).wait_recv()
+        wait_bytes(sum2_recv.at[half], sum_recv.at[1, half])
         total = sum2_send[half, y if half == 0 else z].astype(F32)
         for i in range(3):
             total += sum2_recv[half, i].astype(F32)
-        dw[:, half * 1024 : (half + 1) * 1024] = total
-    arrive(*GRAD)
-
-    for phase in (META, ROW, QKV, DOUT, GRAD):
-        sent(*phase)
-
-    def att_sent(i, _):
-        att_copy(lax.rem(s + i, N)).wait_send()
-        return 0
-
-    lax.fori_loop(1, N, att_sent, 0)
-
-    @pl.when(target_dp != d)
-    def _():
-        att_copy(s).wait_send()
-
-    for i in range(7):
-        gather(d, i, partner).wait_send()
-    for stage in range(2):
-        for half in range(2):
-            for i in range(1, 4):
-                sum_copy(half, stage, i).wait_send()
-
-
-def finish(grads, dw, dquery_early, dkeyval_early, dquery_late, dkeyval_late, dweight):
-    dquery_early[0] = grads[0:NE]
-    dkeyval_early[0] = jnp.stack([grads[NE : 2 * NE], grads[2 * NE : 3 * NE]], axis=1)
-    late = grads[3 * NE : QKV_ROWS].astype(F32)
-    dquery_late[0] = late[0:NL].astype(BF16)
-    dkeyval_late[0] = jnp.stack(
+        dw_v[:, half * 1024 : (half + 1) * 1024] = total
+    dw_copy = pltpu.make_async_copy(dw_v, dw, local_sem.at[0])
+    dw_copy.start()
+    wait_bytes(sum2_recv, sum_send.at[1])
+    for grad, (first, last) in (
+        (GRAD_Q, (0, NE)),
+        (GRAD_LATE, (3 * NE, QKV_ROWS)),
+        (GRAD_KV, (NE, 3 * NE)),
+    ):
+        wait_bytes(dqkv_send.at[1:N, first:last], send.at[grad[0]])
+        arrive(*grad)
+    dw_copy.wait()
+
+
+def finish(
+    grads, dw, dquery_early, dkeyval_early, dquery_late, dkeyval_late, dweight,
+    early_v, query_v, late_v, dw_v, dkve_v, dql_v, dkvl_v, sem,
+):
+    loads = [
+        pltpu.make_async_copy(source, target, sem.at[i])
+        for i, (source, target) in enumerate(
+            (
+                (grads.at[NE : 3 * NE], early_v),
+                (grads.at[3 * NE : QKV_ROWS], late_v),
+                (grads.at[0:NE], query_v.at[0]),
+                (dw, dw_v),
+            )
+        )
+    ]
+    for copy in loads:
+        copy.start()
+    stores = []
+
+    def store(source, target):
+        stores.append(pltpu.make_async_copy(source, target, sem.at[4 + len(stores)]))
+        stores[-1].start()
+
+    loads[0].wait()
+    dkve_v[0] = jnp.stack([early_v[0:NE], early_v[NE : 2 * NE]], axis=1)
+    store(dkve_v, dkeyval_early)
+    loads[1].wait()
+    late = late_v[...].astype(F32)
+    dkvl_v[0] = jnp.stack(
         [late[NL : 2 * NL].astype(BF16), late[2 * NL : 3 * NL].astype(BF16)], axis=1
     )
-    dweight[...] = dw[...]
+    store(dkvl_v, dkeyval_late)
+    dql_v[0] = late[0:NL].astype(BF16)
+    store(dql_v, dquery_late)
+    loads[2].wait()
+    store(query_v, dquery_early)
+    loads[3].wait()
+    store(dw_v, dweight)
+    for copy in stores:
+        copy.wait()
 
 
 def shards(
     depths, owners, cotangent, query_early, keyval_early, query_late, keyval_late, out_weight
 ):
-    vmem = pl.BlockSpec(memory_space=pltpu.VMEM)
     hbm = pl.BlockSpec(memory_space=pl.ANY)
+    results = (
+        jax.ShapeDtypeStruct(query_early.shape, BF16),
+        jax.ShapeDtypeStruct(keyval_early.shape, BF16),
+        jax.ShapeDtypeStruct(query_late.shape, BF16),
+        jax.ShapeDtypeStruct(keyval_late.shape, BF16),
+        jax.ShapeDtypeStruct((N, W), F32),
+    )
     grads, dw = pl.pallas_call(
         kernel,
-        out_shape=(
-            jax.ShapeDtypeStruct((QKV_ROWS, W), BF16),
-            jax.ShapeDtypeStruct((N, W), F32),
-        ),
-        in_specs=[vmem, vmem] + [hbm] * 6,
-        out_specs=(hbm, vmem),
+        out_shape=(jax.ShapeDtypeStruct((QKV_ROWS, W), BF16), results[4]),
+        in_specs=[hbm] * 8,
+        out_specs=(hbm,) * 2,
         scratch_shapes=[
+            pltpu.VMEM((1, TOK), I32),
+            pltpu.VMEM((2, 1, TOK), I32),
             pltpu.VMEM((2, TOK, W), BF16),
             pltpu.VMEM((W, W), BF16),
             pltpu.VMEM((1, NL, W), BF16),
@@ -527,19 +583,20 @@
             pltpu.VMEM((2, 3, 4, 16, W // 2), BF16),
             pltpu.VMEM((2, 4, 16, W // 2), BF16),
             pltpu.VMEM((2, 3, 16, W // 2), BF16),
+            pltpu.VMEM((N, W), F32),
             pltpu.VMEM((KE, KE), F32),
             pltpu.VMEM((KE, KE), BF16),
             pltpu.VMEM((KE, KE), BF16),
             pltpu.VMEM((KL, KL), F32),
             pltpu.VMEM((KL, KL), BF16),
             pltpu.VMEM((KL, KL), BF16),
-            pltpu.SemaphoreType.DMA((6,)),
-            pltpu.SemaphoreType.DMA((6, N)),
-            pltpu.SemaphoreType.DMA((6, N)),
-            pltpu.SemaphoreType.DMA((7,)),
-            pltpu.SemaphoreType.DMA((DP,)),
-            pltpu.SemaphoreType.DMA((2, 2, 3)),
-            pltpu.SemaphoreType.DMA((2, 2, 3)),
+            pltpu.SemaphoreType.DMA((8,)),
+            pltpu.SemaphoreType.DMA((8,)),
+            pltpu.SemaphoreType.DMA((8,)),
+            pltpu.SemaphoreType.DMA,
+            pltpu.SemaphoreType.DMA((4,)),
+            pltpu.SemaphoreType.DMA((2,)),
+            pltpu.SemaphoreType.DMA((2, 2)),
         ],
         compiler_params=pltpu.CompilerParams(
             collective_id=0, has_side_effects=True, vmem_limit_bytes=56 * 1024 * 1024
@@ -554,16 +611,20 @@
     )
     return pl.pallas_call(
         finish,
-        out_shape=(
-            jax.ShapeDtypeStruct(query_early.shape, BF16),
-            jax.ShapeDtypeStruct(keyval_early.shape, BF16),
-            jax.ShapeDtypeStruct(query_late.shape, BF16),
-            jax.ShapeDtypeStruct(keyval_late.shape, BF16),
-            jax.ShapeDtypeStruct((N, W), F32),
-        ),
-        in_specs=[vmem] * 2,
-        out_specs=(vmem,) * 5,
-        compiler_params=pltpu.CompilerParams(vmem_limit_bytes=32 * 1024 * 1024),
+        out_shape=results,
+        in_specs=[pl.BlockSpec(memory_space=pltpu.HBM)] * 2,
+        out_specs=(hbm,) * 5,
+        scratch_shapes=[
+            pltpu.VMEM((2 * NE, W), BF16),
+            pltpu.VMEM((1, NE, W), BF16),
+            pltpu.VMEM((80, W), BF16),
+            pltpu.VMEM((N, W), F32),
+            pltpu.VMEM((1, NE, 2, W), BF16),
+            pltpu.VMEM((1, NL, W), BF16),
+            pltpu.VMEM((1, NL, 2, W), BF16),
+            pltpu.SemaphoreType.DMA((9,)),
+        ],
+        compiler_params=pltpu.CompilerParams(vmem_limit_bytes=48 * 1024 * 1024),
         name="outputs",
     )(grads, dw)
 

time: 71.2 us -> 67.8 us (0.952)
  the two profiles are of different devices: /device:TPU:0 before, /device:TPU:1 now
where the time goes in v3:
time: 67.8 us; the launch traced here: 67.6 us
  Pallas kernels  64.9 us (96%)
  local copies, waits for them, and re-layouts  2.08 us (3%)
    pallas_call x1, Pallas kernels, shards(): pl.pallas_call(kernel, out_shape=(jax.ShapeDtypeStruct((QKV_ROWS, W), BF1...  62.5 us
    pallas_call x1, Pallas kernels, shards(): pl.pallas_call(finish, out_shape=results, in_specs=[pl.BlockSpec(memory_s...  2.43 us
    unnamed x4, local copies, waits for them, and re-layouts  2.08 us

profile of v3, /device:TPU:1, one launch (start us, length us, event | category | flops | bytes accessed | tf_op | source)
XLA Modules:
  0.0 67.6 jit_solution(7415479880916183251)
XLA Ops:
  0.6 62.5 %rows_attention_weight.1 = (bf16[224,2048]{1,0:T(8,128)(2,1)}, f32[16,2048]{1,0:T(8,128)}) custom-call(s32[1,256]{1,0:T(1,128)} %depths.1, s32[2,1,256]{2,1,0:T(1,128)} %owners.1, bf16[2,256,2048]{2,1,0:T(8,128)(2,1)} %bitcast.1, bf16[1,48,2048]{2,1,0:T(8,128)(2,1)} %query_early.1, bf16[1,48,2,2048]{3,2,1,0:T(2,128)(2,1)} %keyval_early.1, ...), custom_call_target="tpu_custom_call" | custom-call | flops 3000000000 | bytes 20000000 | tf_op jit(solution)/shard_map/rows_attention_weight/pallas_call | solution.py:557
  63.1 0.0 copy-start
  63.1 1.2 %copy-done = bf16[224,2048]{1,0:T(8,128)(2,1)S(1)} copy-done((bf16[224,2048]{1,0:T(8,128)(2,1)S(1)}, bf16[224,2048]{1,0:T(8,128)(2,1)}, u32[]{:S(2)}) %copy-start) | copy-done | bytes 917528
  64.3 0.0 copy-start.1
  64.3 0.9 %copy-done.1 = f32[16,2048]{1,0:T(8,128)S(1)} copy-done((f32[16,2048]{1,0:T(8,128)S(1)}, f32[16,2048]{1,0:T(8,128)}, u32[]{:S(2)}) %copy-start.1) | copy-done | bytes 131096
  65.2 2.4 %outputs.1 = (bf16[1,48,2048]{2,1,0:T(8,128)(2,1)}, bf16[1,48,2,2048]{3,2,1,0:T(2,128)(2,1)}, bf16[1,24,2048]{2,1,0:T(8,128)(2,1)}, bf16[1,24,2,2048]{3,2,1,0:T(2,128)(2,1)}, f32[16,2048]{1,0:T(8,128)}) custom-call(bf16[224,2048]{1,0:T(8,128)(2,1)S(1)} %copy-done, f32[16,2048]{1,0:T(8,128)S(1)} %copy-done.1), custom_call_target="tpu_custom_call" | custom-call | tf_op jit(solution)/shard_map/outputs/pallas_call | solution.py:612
Async XLA Ops:
  63.1 1.2 %copy-start = (bf16[224,2048]{1,0:T(8,128)(2,1)S(1)}, bf16[224,2048]{1,0:T(8,128)(2,1)}, u32[]{:S(2)}) copy-start(bf16[224,2048]{1,0:T(8,128)(2,1)} %get-tuple-element.7.grads) | copy-start | bytes 2752516
  64.3 0.9 %copy-start.1 = (f32[16,2048]{1,0:T(8,128)S(1)}, f32[16,2048]{1,0:T(8,128)}, u32[]{:S(2)}) copy-start(f32[16,2048]{1,0:T(8,128)} %get-tuple-element.8.dw) | copy-start | bytes 393220

commit v4 on v3

--- a/solution.py
+++ b/solution.py
@@ -47,12 +47,12 @@
 
 def kernel(
     depths, owners, cot, query_early, keyval_early, query_late, keyval_late, weight,
-    out, dw,
+    dquery_early, dkeyval_early, dquery_late, dkeyval_late, dw,
     depth_v, owner_v, cotv, wv, ql_v, kve_v, kvl_v, qkv_send,
     rows_send, rows_recv, meta_send, meta_recv, qkv_recv, rows_all,
     dout_send, dout_recv, att_send, att_recv, dqkv_send,
     sum1_send, sum1_recv, sum2_send, sum2_recv,
-    dw_v,
+    out, dkve_v, dql_v, dkvl_v, dw_v,
     probs_e, probs_bf_e, ds_e, probs_l, probs_bf_l, ds_l,
     local_sem, send, recv, gsend, grecv, sum_send, sum_recv,
 ):
@@ -89,10 +89,8 @@
         pltpu.make_async_copy(keyval_late, kvl_v, local_sem.at[3]),
         pltpu.make_async_copy(query_early.at[0], qkv_send.at[0:NE], local_sem.at[4]),
     ]
-    for copy in routing + operands:
+    for copy in routing + [cot_copy] + operands + [weight_copy]:
         copy.start()
-    cot_copy.start()
-    weight_copy.start()
 
     barrier = pltpu.get_barrier_semaphore()
 
@@ -139,17 +137,6 @@
     meta_l = dot_nt(token, onehot((line == owner_l * 4 + rank_l) & active_l))
     meta_send[...] = jnp.where(iota((8, E), 0) < 4, meta_e, meta_l)
 
-    for copy in operands:
-        copy.wait()
-    qkv_send[NE : 2 * NE] = kve_v[0, :, 0, :]
-    qkv_send[2 * NE : 3 * NE] = kve_v[0, :, 1, :]
-    for c in range(4):
-        cut = slice(c * 512, (c + 1) * 512)
-        pair = kvl_v[0, :, :, cut].astype(F32)
-        qkv_send[3 * NE : QKV_ROWS, cut] = jnp.concatenate(
-            [ql_v[0, :, cut].astype(F32), pair[:, 0], pair[:, 1], jnp.zeros((8, 512), F32)], axis=0
-        ).astype(BF16)
-
     cot_copy.wait()
     line = iota((TOK, TOK), 0)
     base = jnp.where(active_e, owner_e * 16 + rank_e, -64)
@@ -214,6 +201,16 @@
 
     exchange(*META)
     exchange(*ROW)
+    for copy in operands:
+        copy.wait()
+    qkv_send[NE : 2 * NE] = kve_v[0, :, 0, :]
+    qkv_send[2 * NE : 3 * NE] = kve_v[0, :, 1, :]
+    for c in range(4):
+        cut = slice(c * 512, (c + 1) * 512)
+        pair = kvl_v[0, :, :, cut].astype(F32)
+        qkv_send[3 * NE : QKV_ROWS, cut] = jnp.concatenate(
+            [ql_v[0, :, cut].astype(F32), pair[:, 0], pair[:, 1], jnp.zeros((8, 512), F32)], axis=0
+        ).astype(BF16)
     exchange(*QKV)
 
     arrive(*META)
@@ -482,14 +479,34 @@
     wait_bytes(rows_all.at[1:DP], gsend)
     wait_bytes(sum1_recv, sum_send.at[0])
 
+    writes = []
+
+    def write(source, target):
+        writes.append(pltpu.make_async_copy(source, target, local_sem.at[len(writes)]))
+        writes[-1].start()
+
+    arrive(*GRAD_Q)
+    write(out.at[0:NE], dquery_early.at[0])
+    arrive(*GRAD_LATE)
+    for c in range(4):
+        cut = slice(c * 512, (c + 1) * 512)
+        wide = out[3 * NE : QKV_ROWS, cut].astype(F32)
+        dql_v[0, :, cut] = wide[0:NL].astype(BF16)
+        dkvl_v[0, :, :, cut] = jnp.stack(
+            [wide[NL : 2 * NL].astype(BF16), wide[2 * NL : 3 * NL].astype(BF16)], axis=1
+        )
+    write(dql_v, dquery_late)
+    write(dkvl_v, dkeyval_late)
+    arrive(*GRAD_KV)
+    dkve_v[0] = jnp.stack([out[NE : 2 * NE], out[2 * NE : 3 * NE]], axis=1)
+    write(dkve_v, dkeyval_early)
     for half in range(2):
         wait_bytes(sum2_recv.at[half], sum_recv.at[1, half])
         total = sum2_send[half, y if half == 0 else z].astype(F32)
         for i in range(3):
             total += sum2_recv[half, i].astype(F32)
         dw_v[:, half * 1024 : (half + 1) * 1024] = total
-    dw_copy = pltpu.make_async_copy(dw_v, dw, local_sem.at[0])
-    dw_copy.start()
+    write(dw_v, dw)
     wait_bytes(sum2_recv, sum_send.at[1])
     for grad, (first, last) in (
         (GRAD_Q, (0, NE)),
@@ -497,48 +514,19 @@
         (GRAD_KV, (NE, 3 * NE)),
     ):
         wait_bytes(dqkv_send.at[1:N, first:last], send.at[grad[0]])
-        arrive(*grad)
-    dw_copy.wait()
-
-
-def finish(
-    grads, dw, dquery_early, dkeyval_early, dquery_late, dkeyval_late, dweight,
-    early_v, query_v, late_v, dw_v, dkve_v, dql_v, dkvl_v, sem,
-):
-    loads = [
-        pltpu.make_async_copy(source, target, sem.at[i])
-        for i, (source, target) in enumerate(
-            (
-                (grads.at[NE : 3 * NE], early_v),
-                (grads.at[3 * NE : QKV_ROWS], late_v),
-                (grads.at[0:NE], query_v.at[0]),
-                (dw, dw_v),
-            )
-        )
-    ]
+    for copy in writes:
+        copy.wait()
+
+
+def finish(*refs):
+    sources, targets, held, sem = refs[0:5], refs[5:10], refs[10:15], refs[15]
+    loads = [pltpu.make_async_copy(sources[i], held[i], sem.at[i]) for i in range(5)]
+    stores = [pltpu.make_async_copy(held[i], targets[i], sem.at[5 + i]) for i in range(5)]
     for copy in loads:
         copy.start()
-    stores = []
-
-    def store(source, target):
-        stores.append(pltpu.make_async_copy(source, target, sem.at[4 + len(stores)]))
-        stores[-1].start()
-
-    loads[0].wait()
-    dkve_v[0] = jnp.stack([early_v[0:NE], early_v[NE : 2 * NE]], axis=1)
-    store(dkve_v, dkeyval_early)
-    loads[1].wait()
-    late = late_v[...].astype(F32)
-    dkvl_v[0] = jnp.stack(
-        [late[NL : 2 * NL].astype(BF16), late[2 * NL : 3 * NL].astype(BF16)], axis=1
-    )
-    store(dkvl_v, dkeyval_late)
-    dql_v[0] = late[0:NL].astype(BF16)
-    store(dql_v, dquery_late)
-    loads[2].wait()
-    store(query_v, dquery_early)
-    loads[3].wait()
-    store(dw_v, dweight)
+    for load, store in zip(loads, stores, strict=True):
+        load.wait()
+        store.start()
     for copy in stores:
         copy.wait()
 
@@ -554,11 +542,11 @@
         jax.ShapeDtypeStruct(keyval_late.shape, BF16),
         jax.ShapeDtypeStruct((N, W), F32),
     )
-    grads, dw = pl.pallas_call(
+    outputs = pl.pallas_call(
         kernel,
-        out_shape=(jax.ShapeDtypeStruct((QKV_ROWS, W), BF16), results[4]),
+        out_shape=results,
         in_specs=[hbm] * 8,
-        out_specs=(hbm,) * 2,
+        out_specs=(hbm,) * 5,
         scratch_shapes=[
             pltpu.VMEM((1, TOK), I32),
             pltpu.VMEM((2, 1, TOK), I32),
@@ -583,6 +571,10 @@
             pltpu.VMEM((2, 3, 4, 16, W // 2), BF16),
             pltpu.VMEM((2, 4, 16, W // 2), BF16),
             pltpu.VMEM((2, 3, 16, W // 2), BF16),
+            pltpu.VMEM((QKV_ROWS, W), BF16),
+            pltpu.VMEM((1, NE, 2, W), BF16),
+            pltpu.VMEM((1, NL, W), BF16),
+            pltpu.VMEM((1, NL, 2, W), BF16),
             pltpu.VMEM((N, W), F32),
             pltpu.VMEM((KE, KE), F32),
             pltpu.VMEM((KE, KE), BF16),
@@ -612,21 +604,13 @@
     return pl.pallas_call(
         finish,
         out_shape=results,
-        in_specs=[pl.BlockSpec(memory_space=pltpu.HBM)] * 2,
+        in_specs=[hbm] * 5,
         out_specs=(hbm,) * 5,
-        scratch_shapes=[
-            pltpu.VMEM((2 * NE, W), BF16),
-            pltpu.VMEM((1, NE, W), BF16),
-            pltpu.VMEM((80, W), BF16),
-            pltpu.VMEM((N, W), F32),
-            pltpu.VMEM((1, NE, 2, W), BF16),
-            pltpu.VMEM((1, NL, W), BF16),
-            pltpu.VMEM((1, NL, 2, W), BF16),
-            pltpu.SemaphoreType.DMA((9,)),
-        ],
-        compiler_params=pltpu.CompilerParams(vmem_limit_bytes=48 * 1024 * 1024),
+        scratch_shapes=[pltpu.VMEM(result.shape, result.dtype) for result in results]
+        + [pltpu.SemaphoreType.DMA((10,))],
+        compiler_params=pltpu.CompilerParams(vmem_limit_bytes=56 * 1024 * 1024),
         name="outputs",
-    )(grads, dw)
+    )(*outputs)
 
 
 def solution(mesh):

time: 67.8 us -> 62.8 us (0.926)
  the two profiles are of different devices: /device:TPU:1 before, /device:TPU:0 now
where the time goes in v4:
time: 62.8 us; the launch traced here: 62.4 us
  Pallas kernels  61.8 us (98%)
  between operations  0.64 us (1%)
    pallas_call x1, Pallas kernels, shards(): pl.pallas_call(kernel, out_shape=results, in_specs=[hbm] * 8, out_specs=(...  59.7 us
    pallas_call x1, Pallas kernels, shards(): pl.pallas_call(finish, out_shape=results, in_specs=[hbm] * 5, out_specs=(...  2.07 us

profile of v4, /device:TPU:0, one launch (start us, length us, event | category | flops | bytes accessed | tf_op | source)
XLA Modules:
  0.0 62.4 jit_solution(11871717767631221808)
XLA Ops:
  0.6 59.7 %rows_attention_weight.1 = (bf16[1,48,2048]{2,1,0:T(8,128)(2,1)}, bf16[1,48,2,2048]{3,2,1,0:T(2,128)(2,1)}, bf16[1,24,2048]{2,1,0:T(8,128)(2,1)}, bf16[1,24,2,2048]{3,2,1,0:T(2,128)(2,1)}, f32[16,2048]{1,0:T(8,128)}) custom-call(s32[1,256]{1,0:T(1,128)} %depths.1, s32[2,1,256]{2,1,0:T(1,128)} %owners.1, bf16[2,256,2048]{2,1,0:T(8,128)(2,1)} %bitcast.1, ...), custom_call_target="tpu_custom_call" | custom-call | flops 3000000000 | bytes 20000000 | tf_op jit(solution)/shard_map/rows_attention_weight/pallas_call | solution.py:545
  60.4 2.1 %outputs.1 = (bf16[1,48,2048]{2,1,0:T(8,128)(2,1)}, bf16[1,48,2,2048]{3,2,1,0:T(2,128)(2,1)}, bf16[1,24,2048]{2,1,0:T(8,128)(2,1)}, bf16[1,24,2,2048]{3,2,1,0:T(2,128)(2,1)}, f32[16,2048]{1,0:T(8,128)}) custom-call(bf16[1,48,2048]{2,1,0:T(8,128)(2,1)} %get-tuple-element.10.refs_0_, bf16[1,48,2,2048]{3,2,1,0:T(2,128)(2,1)} %get-tuple-element.11.refs_1_, ...), custom_call_target="tpu_custom_call" | custom-call | tf_op jit(solution)/shard_map/outputs/pallas_call | solution.py:604

commit v5 on v4

--- a/solution.py
+++ b/solution.py
@@ -16,7 +16,8 @@
 NE, NL = 48, 24
 NLP = 32
 ROWS = NE + NLP
-QKV_ROWS = 3 * NE + 80
+GRAD_ROWS = 3 * NE + 80
+QKV_ROWS = 3 * NE + 64
 OTHERS = (
     (2, 2), (1, 2), (2, 1), (2, 3), (3, 2), (0, 2), (2, 0), (1, 1),
     (3, 3), (1, 3), (3, 1), (0, 1), (1, 0), (0, 3), (3, 0),
@@ -66,10 +67,6 @@
     def head_of(j):
         return lax.rem(chip + lax.div(j, 4) + 2 * core, 4) * 4 + lax.rem(j, 4)
 
-    def holder(of_dp, head):
-        turn = lax.div(head, 4) + 8 - lax.div(of_dp, 2) - 2 * lax.rem(of_dp, 2)
-        return lax.rem(turn, 4) * 4 + lax.rem(head, 4)
-
     def same_core(i):
         return lax.rem(chip + i, 4) * 2 + core
 
@@ -83,13 +80,13 @@
         pltpu.make_async_copy(depths, depth_v, local_sem.at[6]),
         pltpu.make_async_copy(owners, owner_v, local_sem.at[7]),
     ]
+    late_copy = pltpu.make_async_copy(keyval_late, kvl_v, local_sem.at[3])
     operands = [
         pltpu.make_async_copy(keyval_early, kve_v, local_sem.at[2]),
         pltpu.make_async_copy(query_late, ql_v, local_sem.at[5]),
-        pltpu.make_async_copy(keyval_late, kvl_v, local_sem.at[3]),
         pltpu.make_async_copy(query_early.at[0], qkv_send.at[0:NE], local_sem.at[4]),
     ]
-    for copy in routing + [cot_copy] + operands + [weight_copy]:
+    for copy in routing + [late_copy, cot_copy] + operands + [weight_copy]:
         copy.start()
 
     barrier = pltpu.get_barrier_semaphore()
@@ -97,26 +94,19 @@
     def greet(to_dp, to_seq):
         pl.semaphore_signal(barrier, inc=1, device_id=(to_dp, to_seq), device_id_type=MESH)
 
-    def greet_seq(i, _):
+    for i in range(1, N):
         greet(d, lax.rem(s + i, N))
-        return 0
-
-    lax.fori_loop(1, N, greet_seq, 0)
     greet(partner, s)
     for i in (1, 3):
         greet(same_core(i), s)
-
-    def greet_heads(i, _):
-        from_dp = lax.div(i, 2)
-        from_seq = holder(from_dp, 2 * d + lax.rem(i, 2))
-
-        @pl.when(jnp.logical_or(from_dp != d, from_seq != s))
-        def _():
-            greet(from_dp, from_seq)
-
-        return 0
-
-    lax.fori_loop(0, 2 * DP, greet_heads, 0)
+    for from_dp in range(DP):
+        turn = lax.rem(chip + 8 - from_dp // 2 - 2 * (from_dp % 2), 4)
+        for p in range(2):
+            from_seq = turn * 4 + 2 * core + p
+
+            @pl.when(jnp.logical_or(d != from_dp, from_seq != s))
+            def _(from_dp=from_dp, from_seq=from_seq):
+                greet(from_dp, from_seq)
 
     for copy in routing:
         copy.wait()
@@ -135,7 +125,11 @@
     line = iota((E, TOK), 0)
     meta_e = dot_nt(token, onehot((line == owner_e * 8 + rank_e) & active_e))
     meta_l = dot_nt(token, onehot((line == owner_l * 4 + rank_l) & active_l))
-    meta_send[...] = jnp.where(iota((8, E), 0) < 4, meta_e, meta_l)
+    meta = jnp.where(iota((8, E), 0) < 4, meta_e, meta_l)
+    late_copy.wait()
+    meta_send[...] = jnp.concatenate(
+        [kvl_v[0, 16:NL, 1, :].astype(F32), jnp.concatenate([meta] * N, axis=1)], axis=0
+    ).astype(BF16)
 
     cot_copy.wait()
     line = iota((TOK, TOK), 0)
@@ -182,7 +176,7 @@
     def columns(ref, j):
         return ref.at[:, pl.ds(pl.multiple_of(head_of(j) * E, E), E)]
 
-    META = (0, lambda j: meta_send, lambda j: meta_recv.at[j], meta_recv)
+    META = (0, lambda j: columns(meta_send, j), lambda j: meta_recv.at[j], meta_recv)
     ROW = (1, lambda j: rows_send.at[j], lambda j: rows_recv.at[j], rows_recv)
     QKV = (2, lambda j: columns(qkv_send, j), lambda j: qkv_recv.at[j], qkv_recv)
     DOUT = (3, lambda j: columns(dout_send, j), lambda j: dout_recv.at[j], dout_recv)
@@ -195,7 +189,7 @@
             out.at[first:last],
         )
 
-    GRAD_Q, GRAD_LATE = grads(4, 0, NE), grads(5, 3 * NE, QKV_ROWS)
+    GRAD_Q, GRAD_LATE = grads(4, 0, NE), grads(5, 3 * NE, GRAD_ROWS)
     GRAD_KV = grads(6, NE, 3 * NE)
     ATT = 7
 
@@ -209,17 +203,19 @@
         cut = slice(c * 512, (c + 1) * 512)
         pair = kvl_v[0, :, :, cut].astype(F32)
         qkv_send[3 * NE : QKV_ROWS, cut] = jnp.concatenate(
-            [ql_v[0, :, cut].astype(F32), pair[:, 0], pair[:, 1], jnp.zeros((8, 512), F32)], axis=0
+            [ql_v[0, :, cut].astype(F32), pair[:, 0], pair[0:16, 1]], axis=0
         ).astype(BF16)
     exchange(*QKV)
 
     arrive(*META)
+
+    tokens = meta_recv[...].astype(F32)
 
     def spread(first, shift):
         lane = iota((N, E), 1)
         mine = (lane >> shift) == iota((N, E), 0)
         wide = jnp.concatenate(
-            [jnp.where(mine, meta_recv[j, first : first + 1], 0.0) for j in range(N)], axis=0
+            [jnp.where(mine, tokens[j, first : first + 1], 0.0) for j in range(N)], axis=0
         )
         low = (1 << shift) - 1
         same = onehot((iota((E, E), 0) & low) == (iota((E, E), 1) & low))
@@ -229,8 +225,8 @@
             total += jnp.where((lane >> shift) == j, wide[j * N : (j + 1) * N], 0.0)
         return total
 
-    token_e = spread(0, 3)
-    token_l = spread(4, 2)
+    token_e = spread(8, 3)
+    token_l = spread(12, 2)
 
     def tables(token, shift, slots, padded):
         peak = 1 << shift
@@ -358,7 +354,9 @@
         probs_bf_e[b * 192 : (b + 1) * 192] = probs_bf
         att_send[4 * b : 4 * b + 4, 0:NE, :] = attended.reshape(4, NE, E).astype(BF16)
     attended_out(0, NE)
-    wide = qkv_recv[:, 3 * NE : QKV_ROWS, :].astype(F32)
+    wide = jnp.concatenate(
+        [qkv_recv[:, 3 * NE : QKV_ROWS, :].astype(F32), meta_recv[:, 0:8, :].astype(F32)], axis=1
+    )
     query_l, key_l, value_l = (late(wide, part).astype(BF16) for part in range(3))
     gap = jnp.zeros((8, NLP - NL, E), F32)
     for b in range(2):
@@ -411,26 +409,12 @@
     dvalue = dot_tn(probs_bf_l[...], dout_l)
     parts = [part.reshape(N, NL, E) for part in (dquery, dkey, dvalue)]
     parts.append(jnp.zeros((N, 8, E), F32))
-    dqkv_send[:, 3 * NE : QKV_ROWS, :] = jnp.concatenate(parts, axis=1).astype(BF16)
+    dqkv_send[:, 3 * NE : GRAD_ROWS, :] = jnp.concatenate(parts, axis=1).astype(BF16)
     exchange(*GRAD_LATE)
     gather_far()
 
     wait_bytes(att_recv, recv.at[ATT])
     wait_bytes(rows_all.at[0:4], grecv.at[FROM_PARTNER])
-    rows = rows_all[...].reshape(DP * ROWS, W)
-    for p in range(2):
-        attended = att_recv[:, p].reshape(DP * ROWS, E)
-        for c in range(4):
-            half, cut = c // 2, slice((c % 2) * 512, (c % 2) * 512 + 512)
-            part = dot_tn(attended, rows[:, c * 512 : (c + 1) * 512])
-            part = part.reshape(2, 4, 16, 512).astype(BF16)
-            if half == 0:
-                sum1_send[0, 2 * p : 2 * p + 2, :, :, cut] = part
-            else:
-                for i in range(2):
-                    for j in range(4):
-                        sum1_send[1, j, 2 * p + i, :, cut] = part[i, j]
-
     def along(half, stage, i):
         if half == stage:
             to = lax.rem(z + i, 4)
@@ -450,8 +434,21 @@
             device_id_type=MESH,
         )
 
-    for i in (2, 1, 3):
-        for half in range(2):
+    rows = rows_all[...].reshape(DP * ROWS, W)
+    columns_of = [att_recv[:, p].reshape(DP * ROWS, E) for p in range(2)]
+    for half in range(2):
+        for p in range(2):
+            for c in range(2):
+                cut, first = slice(c * 512, (c + 1) * 512), half * 1024 + c * 512
+                part = dot_tn(columns_of[p], rows[:, first : first + 512])
+                part = part.reshape(2, 4, 16, 512).astype(BF16)
+                if half == 0:
+                    sum1_send[0, 2 * p : 2 * p + 2, :, :, cut] = part
+                else:
+                    for i in range(2):
+                        for j in range(4):
+                            sum1_send[1, j, 2 * p + i, :, cut] = part[i, j]
+        for i in (2, 1, 3):
             sum_copy(half, 0, i).start()
     exchange(*GRAD_KV)
     for half in range(2):
@@ -490,7 +487,7 @@
     arrive(*GRAD_LATE)
     for c in range(4):
         cut = slice(c * 512, (c + 1) * 512)
-        wide = out[3 * NE : QKV_ROWS, cut].astype(F32)
+        wide = out[3 * NE : GRAD_ROWS, cut].astype(F32)
         dql_v[0, :, cut] = wide[0:NL].astype(BF16)
         dkvl_v[0, :, :, cut] = jnp.stack(
             [wide[NL : 2 * NL].astype(BF16), wide[2 * NL : 3 * NL].astype(BF16)], axis=1
@@ -510,7 +507,7 @@
     wait_bytes(sum2_recv, sum_send.at[1])
     for grad, (first, last) in (
         (GRAD_Q, (0, NE)),
-        (GRAD_LATE, (3 * NE, QKV_ROWS)),
+        (GRAD_LATE, (3 * NE, GRAD_ROWS)),
         (GRAD_KV, (NE, 3 * NE)),
     ):
         wait_bytes(dqkv_send.at[1:N, first:last], send.at[grad[0]])
@@ -558,20 +555,20 @@
             pltpu.VMEM((QKV_ROWS, W), BF16),
             pltpu.VMEM((N, 16, 1536), BF16),
             pltpu.VMEM((N, 16, 1536), BF16),
-            pltpu.VMEM((8, E), F32),
-            pltpu.VMEM((N, 8, E), F32),
+            pltpu.VMEM((16, W), BF16),
+            pltpu.VMEM((N, 16, E), BF16),
             pltpu.VMEM((N, QKV_ROWS, E), BF16),
             pltpu.VMEM((DP, ROWS, W), BF16),
             pltpu.VMEM((ROWS, W), BF16),
             pltpu.VMEM((N, ROWS, E), BF16),
             pltpu.VMEM((N, ROWS, E), BF16),
             pltpu.VMEM((DP, 2, ROWS, E), BF16),
-            pltpu.VMEM((N, QKV_ROWS, E), BF16),
+            pltpu.VMEM((N, GRAD_ROWS, E), BF16),
             pltpu.VMEM((2, 4, 4, 16, W // 2), BF16),
             pltpu.VMEM((2, 3, 4, 16, W // 2), BF16),
             pltpu.VMEM((2, 4, 16, W // 2), BF16),
             pltpu.VMEM((2, 3, 16, W // 2), BF16),
-            pltpu.VMEM((QKV_ROWS, W), BF16),
+            pltpu.VMEM((GRAD_ROWS, W), BF16),
             pltpu.VMEM((1, NE, 2, W), BF16),
             pltpu.VMEM((1, NL, W), BF16),
             pltpu.VMEM((1, NL, 2, W), BF16),

time: 62.8 us -> 62.7 us (level); the launches traced: 62.4 us -> 61.6 us
  Pallas kernels: 61.8 us -> 61 us
    pallas_call x1, Pallas kernels: 59.7 us -> 58.9 us  [shards(): pl.pallas_call(kernel, out_shape=results, in_specs=[hbm] * 8, out_specs=(...]
where the time goes in v5:
time: 62.7 us; the launch traced here: 61.6 us
  Pallas kernels  61 us (97%)
  between operations  0.64 us (1%)
    pallas_call x1, Pallas kernels, shards(): pl.pallas_call(kernel, out_shape=results, in_specs=[hbm] * 8, out_specs=(...  58.9 us
    pallas_call x1, Pallas kernels, shards(): pl.pallas_call(finish, out_shape=results, in_specs=[hbm] * 5, out_specs=(...  2.07 us

profile of v5, /device:TPU:0, one launch (start us, length us, event | category | flops | bytes accessed | tf_op | source)
XLA Modules:
  0.0 61.6 jit_solution(10370011936743682659)
XLA Ops:
  0.6 58.9 %rows_attention_weight.1 = (bf16[1,48,2048]{2,1,0:T(8,128)(2,1)}, bf16[1,48,2,2048]{3,2,1,0:T(2,128)(2,1)}, bf16[1,24,2048]{2,1,0:T(8,128)(2,1)}, bf16[1,24,2,2048]{3,2,1,0:T(2,128)(2,1)}, f32[16,2048]{1,0:T(8,128)}) custom-call(s32[1,256]{1,0:T(1,128)} %depths.1, s32[2,1,256]{2,1,0:T(1,128)} %owners.1, bf16[2,256,2048]{2,1,0:T(8,128)(2,1)} %bitcast.1, ...), custom_call_target="tpu_custom_call" | custom-call | flops 3000000000 | bytes 20000000 | tf_op jit(solution)/shard_map/rows_attention_weight/pallas_call | solution.py:542
  59.6 2.1 %outputs.1 = (bf16[1,48,2048]{2,1,0:T(8,128)(2,1)}, bf16[1,48,2,2048]{3,2,1,0:T(2,128)(2,1)}, bf16[1,24,2048]{2,1,0:T(8,128)(2,1)}, bf16[1,24,2,2048]{3,2,1,0:T(2,128)(2,1)}, f32[16,2048]{1,0:T(8,128)}) custom-call(bf16[1,48,2048]{2,1,0:T(8,128)(2,1)} %get-tuple-element.10.refs_0_, bf16[1,48,2,2048]{3,2,1,0:T(2,128)(2,1)} %get-tuple-element.11.refs_1_, ...), custom_call_target="tpu_custom_call" | custom-call | tf_op jit(solution)/shard_map/outputs/pallas_call | solution.py:601

commit v6 on v5

--- a/solution.py
+++ b/solution.py
@@ -48,12 +48,12 @@
 
 def kernel(
     depths, owners, cot, query_early, keyval_early, query_late, keyval_late, weight,
-    dquery_early, dkeyval_early, dquery_late, dkeyval_late, dw,
+    dquery_early, dkeyval_early, dquery_late, dkeyval_late, sums,
     depth_v, owner_v, cotv, wv, ql_v, kve_v, kvl_v, qkv_send,
     rows_send, rows_recv, meta_send, meta_recv, qkv_recv, rows_all,
     dout_send, dout_recv, att_send, att_recv, dqkv_send,
-    sum1_send, sum1_recv, sum2_send, sum2_recv,
-    out, dkve_v, dql_v, dkvl_v, dw_v,
+    sum1_send, sum1_recv, sum2_send,
+    out, dkve_v, dql_v, dkvl_v,
     probs_e, probs_bf_e, ds_e, probs_l, probs_bf_l, ds_l,
     local_sem, send, recv, gsend, grecv, sum_send, sum_recv,
 ):
@@ -74,7 +74,14 @@
     target_dp = lax.div(my_head, 2)
     parity = lax.rem(my_head, 2)
 
-    cot_copy = pltpu.make_async_copy(cot, cotv, local_sem.at[0])
+    cot_copies = [
+        pltpu.make_async_copy(
+            cot.at[r, 0, pl.ds(i * 128, 128)], cotv.at[r, pl.ds(i * 128, 128)],
+            local_sem.at[8 + 2 * r + i],
+        )
+        for r in range(2)
+        for i in range(2)
+    ]
     weight_copy = pltpu.make_async_copy(weight, wv, local_sem.at[1])
     routing = [
         pltpu.make_async_copy(depths, depth_v, local_sem.at[6]),
@@ -86,7 +93,7 @@
         pltpu.make_async_copy(query_late, ql_v, local_sem.at[5]),
         pltpu.make_async_copy(query_early.at[0], qkv_send.at[0:NE], local_sem.at[4]),
     ]
-    for copy in routing + [late_copy, cot_copy] + operands + [weight_copy]:
+    for copy in routing + [late_copy] + cot_copies + operands + [weight_copy]:
         copy.start()
 
     barrier = pltpu.get_barrier_semaphore()
@@ -131,12 +138,15 @@
         [kvl_v[0, 16:NL, 1, :].astype(F32), jnp.concatenate([meta] * N, axis=1)], axis=0
     ).astype(BF16)
 
-    cot_copy.wait()
+    for copy in cot_copies[0:2]:
+        copy.wait()
     line = iota((TOK, TOK), 0)
     base = jnp.where(active_e, owner_e * 16 + rank_e, -64)
     packed = dot(onehot(line == base), cotv[0, :, 0:1024])
     packed += dot(onehot(line == base + 8), cotv[0, :, 1024:2048])
     rows_send[:, :, 0:1024] = packed.reshape(N, 16, 1024).astype(BF16)
+    for copy in cot_copies[2:4]:
+        copy.wait()
     base = jnp.where(active_l, owner_l * 16 + rank_l, -64)
     packed = dot(onehot(line == base), cotv[1, :, 0:512])
     for q in range(1, 4):
@@ -189,9 +199,15 @@
             out.at[first:last],
         )
 
-    GRAD_Q, GRAD_LATE = grads(4, 0, NE), grads(5, 3 * NE, GRAD_ROWS)
-    GRAD_KV = grads(6, NE, 3 * NE)
-    ATT = 7
+    GRAD_Q = (
+        4,
+        lambda j: dqkv_send.at[j, 0:NE],
+        lambda j: columns(dquery_early.at[0], j),
+        dquery_early.at[0],
+    )
+    GRAD_LATE = grads(5, 3 * NE, GRAD_ROWS)
+    GRAD_K, GRAD_V = grads(6, NE, 2 * NE), grads(7, 2 * NE, 3 * NE)
+    ATT = 8
 
     exchange(*META)
     exchange(*ROW)
@@ -311,7 +327,6 @@
     exchange(*DOUT)
 
     arrive(*QKV)
-    gather_near()
 
     def late(wide, part):
         return wide[:, part * NL : (part + 1) * NL].reshape(KL, E)
@@ -354,6 +369,7 @@
         probs_bf_e[b * 192 : (b + 1) * 192] = probs_bf
         att_send[4 * b : 4 * b + 4, 0:NE, :] = attended.reshape(4, NE, E).astype(BF16)
     attended_out(0, NE)
+    gather_near()
     wide = jnp.concatenate(
         [qkv_recv[:, 3 * NE : QKV_ROWS, :].astype(F32), meta_recv[:, 0:8, :].astype(F32)], axis=1
     )
@@ -370,6 +386,11 @@
     attended_out(NE, ROWS)
 
     arrive(*DOUT)
+    dout_e = dout_recv[:, 0:NE, :].reshape(KE, E)
+    for c in range(2):
+        dvalue = dot_tn(probs_bf_e[:, c * 384 : (c + 1) * 384], dout_e)
+        dqkv_send[8 * c : 8 * c + 8, 2 * NE : 3 * NE, :] = dvalue.reshape(8, NE, E).astype(BF16)
+    exchange(*GRAD_V)
 
     def backward(query, key, value, dout, attended, probs):
         delta = jnp.sum(dout.astype(F32) * attended.astype(F32), axis=1, keepdims=True)
@@ -386,7 +407,11 @@
         )
         ds_e[b * 192 : (b + 1) * 192] = dscores
         dqkv_send[4 * b : 4 * b + 4, 0:NE, :] = dquery.reshape(4, NE, E).astype(BF16)
-    exchange(*GRAD_Q)
+    query_e = qkv_recv[:, 0:NE, :].reshape(KE, E)
+    for c in range(2):
+        dkey = dot_tn(ds_e[:, c * 384 : (c + 1) * 384], query_e) * SCALE
+        dqkv_send[8 * c : 8 * c + 8, NE : 2 * NE, :] = dkey.reshape(8, NE, E).astype(BF16)
+    exchange(*GRAD_K)
     dout_l = late(dout_recv[:, NE:ROWS, :].astype(F32), 0).astype(BF16)
     attended_l = late(att_send[:, NE:ROWS, :].astype(F32), 0)
     dquery_l = []
@@ -397,13 +422,6 @@
         )
         ds_l[b * 192 : (b + 1) * 192] = dscores
         dquery_l.append(dquery)
-    query_e = qkv_recv[:, 0:NE, :].reshape(KE, E)
-    dout_e = dout_recv[:, 0:NE, :].reshape(KE, E)
-    for c in range(2):
-        dkey = dot_tn(ds_e[:, c * 384 : (c + 1) * 384], query_e) * SCALE
-        dqkv_send[8 * c : 8 * c + 8, NE : 2 * NE, :] = dkey.reshape(8, NE, E).astype(BF16)
-        dvalue = dot_tn(probs_bf_e[:, c * 384 : (c + 1) * 384], dout_e)
-        dqkv_send[8 * c : 8 * c + 8, 2 * NE : 3 * NE, :] = dvalue.reshape(8, NE, E).astype(BF16)
     dquery = jnp.concatenate(dquery_l, axis=0)
     dkey = dot_tn(ds_l[...], query_l) * SCALE
     dvalue = dot_tn(probs_bf_l[...], dout_l)
@@ -423,7 +441,7 @@
         return to, z * 4 + to
 
     def sum_copy(half, stage, i):
-        source, target = (sum1_send, sum1_recv) if stage == 0 else (sum2_send, sum2_recv)
+        source, target = (sum1_send, sum1_recv) if stage == 0 else (sum2_send, sums)
         to, device = along(half, stage, i)
         return pltpu.make_async_remote_copy(
             src_ref=source.at[half, to],
@@ -450,7 +468,7 @@
                             sum1_send[1, j, 2 * p + i, :, cut] = part[i, j]
         for i in (2, 1, 3):
             sum_copy(half, 0, i).start()
-    exchange(*GRAD_KV)
+    exchange(*GRAD_Q)
     for half in range(2):
         wait_bytes(sum1_recv.at[half], sum_recv.at[0, half])
         total = sum1_send[half, z if half == 0 else y].astype(F32)
@@ -459,6 +477,8 @@
         sum2_send[half] = total.astype(BF16)
         for i in (2, 1, 3):
             sum_copy(half, 1, i).start()
+        own = sum2_send.at[half, along(half, 1, 0)[0]]
+        pltpu.make_async_copy(own, sums.at[half, 3], sum_recv.at[1, half]).start()
 
     wait_bytes(meta_recv.at[1:N], send.at[META[0]])
     wait_bytes(rows_recv.at[1:N], send.at[ROW[0]])
@@ -482,8 +502,6 @@
         writes.append(pltpu.make_async_copy(source, target, local_sem.at[len(writes)]))
         writes[-1].start()
 
-    arrive(*GRAD_Q)
-    write(out.at[0:NE], dquery_early.at[0])
     arrive(*GRAD_LATE)
     for c in range(4):
         cut = slice(c * 512, (c + 1) * 512)
@@ -494,38 +512,47 @@
         )
     write(dql_v, dquery_late)
     write(dkvl_v, dkeyval_late)
-    arrive(*GRAD_KV)
+    arrive(*GRAD_V)
+    arrive(*GRAD_K)
     dkve_v[0] = jnp.stack([out[NE : 2 * NE], out[2 * NE : 3 * NE]], axis=1)
     write(dkve_v, dkeyval_early)
-    for half in range(2):
-        wait_bytes(sum2_recv.at[half], sum_recv.at[1, half])
-        total = sum2_send[half, y if half == 0 else z].astype(F32)
-        for i in range(3):
-            total += sum2_recv[half, i].astype(F32)
-        dw_v[:, half * 1024 : (half + 1) * 1024] = total
-    write(dw_v, dw)
-    wait_bytes(sum2_recv, sum_send.at[1])
     for grad, (first, last) in (
         (GRAD_Q, (0, NE)),
         (GRAD_LATE, (3 * NE, GRAD_ROWS)),
-        (GRAD_KV, (NE, 3 * NE)),
+        (GRAD_K, (NE, 2 * NE)),
+        (GRAD_V, (2 * NE, 3 * NE)),
     ):
         wait_bytes(dqkv_send.at[1:N, first:last], send.at[grad[0]])
     for copy in writes:
         copy.wait()
+    arrive(*GRAD_Q)
+    wait_bytes(sums.at[:, 0:3], sum_send.at[1])
+    for half in range(2):
+        wait_bytes(sums.at[half], sum_recv.at[1, half])
 
 
 def finish(*refs):
-    sources, targets, held, sem = refs[0:5], refs[5:10], refs[10:15], refs[15]
-    loads = [pltpu.make_async_copy(sources[i], held[i], sem.at[i]) for i in range(5)]
-    stores = [pltpu.make_async_copy(held[i], targets[i], sem.at[5 + i]) for i in range(5)]
-    for copy in loads:
-        copy.start()
-    for load, store in zip(loads, stores, strict=True):
-        load.wait()
-        store.start()
-    for copy in stores:
-        copy.wait()
+    sources, targets, held, dw_v, sem = refs[0:5], refs[5:10], refs[10:15], refs[15], refs[16]
+    order = (4, 1, 3, 0, 2)
+    loads = {i: pltpu.make_async_copy(sources[i], held[i], sem.at[i]) for i in order}
+    stores = {
+        i: pltpu.make_async_copy(dw_v if i == 4 else held[i], targets[i], sem.at[5 + i])
+        for i in order
+    }
+    for i in order:
+        loads[i].start()
+    for i in (1, 3, 0, 2):
+        loads[i].wait()
+        stores[i].start()
+    loads[4].wait()
+    for half in range(2):
+        total = held[4][half, 3].astype(F32)
+        for i in range(3):
+            total += held[4][half, i].astype(F32)
+        dw_v[:, half * 1024 : (half + 1) * 1024] = total
+    stores[4].start()
+    for i in order:
+        stores[i].wait()
 
 
 def shards(
@@ -539,9 +566,10 @@
         jax.ShapeDtypeStruct(keyval_late.shape, BF16),
         jax.ShapeDtypeStruct((N, W), F32),
     )
+    between = results[0:4] + (jax.ShapeDtypeStruct((2, 4, 16, W // 2), BF16),)
     outputs = pl.pallas_call(
         kernel,
-        out_shape=results,
+        out_shape=between,
         in_specs=[hbm] * 8,
         out_specs=(hbm,) * 5,
         scratch_shapes=[
@@ -567,21 +595,19 @@
             pltpu.VMEM((2, 4, 4, 16, W // 2), BF16),
             pltpu.VMEM((2, 3, 4, 16, W // 2), BF16),
             pltpu.VMEM((2, 4, 16, W // 2), BF16),
-            pltpu.VMEM((2, 3, 16, W // 2), BF16),
             pltpu.VMEM((GRAD_ROWS, W), BF16),
             pltpu.VMEM((1, NE, 2, W), BF16),
             pltpu.VMEM((1, NL, W), BF16),
             pltpu.VMEM((1, NL, 2, W), BF16),
-            pltpu.VMEM((N, W), F32),
             pltpu.VMEM((KE, KE), F32),
             pltpu.VMEM((KE, KE), BF16),
             pltpu.VMEM((KE, KE), BF16),
             pltpu.VMEM((KL, KL), F32),
             pltpu.VMEM((KL, KL), BF16),
             pltpu.VMEM((KL, KL), BF16),
-            pltpu.SemaphoreType.DMA((8,)),
-            pltpu.SemaphoreType.DMA((8,)),
-            pltpu.SemaphoreType.DMA((8,)),
+            pltpu.SemaphoreType.DMA((12,)),
+            pltpu.SemaphoreType.DMA((9,)),
+            pltpu.SemaphoreType.DMA((9,)),
             pltpu.SemaphoreType.DMA,
             pltpu.SemaphoreType.DMA((4,)),
             pltpu.SemaphoreType.DMA((2,)),
@@ -595,7 +621,7 @@
         ),
         name="rows_attention_weight",
     )(
-        depths, owners, cotangent[:, 0], query_early, keyval_early, query_late, keyval_late,
+        depths, owners, cotangent, query_early, keyval_early, query_late, keyval_late,
         out_weight,
     )
     return pl.pallas_call(
@@ -603,8 +629,8 @@
         out_shape=results,
         in_specs=[hbm] * 5,
         out_specs=(hbm,) * 5,
-        scratch_shapes=[pltpu.VMEM(result.shape, result.dtype) for result in results]
-        + [pltpu.SemaphoreType.DMA((10,))],
+        scratch_shapes=[pltpu.VMEM(array.shape, array.dtype) for array in between]
+        + [pltpu.VMEM((N, W), F32), pltpu.SemaphoreType.DMA((10,))],
         compiler_params=pltpu.CompilerParams(vmem_limit_bytes=56 * 1024 * 1024),
         name="outputs",
     )(*outputs)

time: 62.7 us -> 62 us (0.989); the launches traced: 61.6 us -> 61.9 us
  no operation moved by 1% of the time
where the time goes in v6:
time: 62 us; the launch traced here: 61.9 us
  Pallas kernels  61.3 us (99%)
  between operations  0.64 us (1%)
    pallas_call x1, Pallas kernels, shards(): pl.pallas_call(kernel, out_shape=between, in_specs=[hbm] * 8, out_specs=(...  59.1 us
    pallas_call x1, Pallas kernels, shards(): pl.pallas_call(finish, out_shape=results, in_specs=[hbm] * 5, out_specs=(...  2.12 us

profile of v6, /device:TPU:0, one launch (start us, length us, event | category | flops | bytes accessed | tf_op | source)
XLA Modules:
  0.0 61.9 jit_solution(14914220124524872426)
XLA Ops:
  0.6 59.1 %rows_attention_weight.1 = (bf16[1,48,2048]{2,1,0:T(8,128)(2,1)}, bf16[1,48,2,2048]{3,2,1,0:T(2,128)(2,1)}, bf16[1,24,2048]{2,1,0:T(8,128)(2,1)}, bf16[1,24,2,20...) custom-call(s32[1,256]{1,0:T(1,128)} %depths.1, s32[2,1,256]{2,1,0:T(1,128)} %owners.1, bf16[2,1,256,2048]{3,2,1,0:T(8,128)(2,1)} %cot.1, ...), custom_call_target="tpu_custom_call" | custom-call | flops 3000000000 | bytes 20000000 | tf_op jit(solution)/shard_map/rows_attention_weight/pallas_call | solution.py:570
  59.8 2.1 %outputs.1 = (bf16[1,48,2048]{2,1,0:T(8,128)(2,1)}, bf16[1,48,2,2048]{3,2,1,0:T(2,128)(2,1)}, bf16[1,24,2048]{2,1,0:T(8,128)(2,1)}, bf16[1,24,2,2048]{3,2,1,0:T(2,128)(2,1)}, f32[16,2048]{1,0:T(8,128)}) custom-call(bf16[1,48,2048]{2,1,0:T(8,128)(2,1)} %get-tuple-element.10.refs_0_, bf16[1,48,2,2048]{3,2,1,0:T(2,128)(2,1)} %get-tuple-element.11.refs_1_, ...), custom_call_target="tpu_custom_call" | custom-call | tf_op jit(solution)/shard_map/outputs/pallas_call | solution.py:627

commit v7 on v6

--- a/solution.py
+++ b/solution.py
@@ -288,10 +288,12 @@
         got = dot(pick, rows_recv[:, :, 1024:1536].reshape(TOK, 512))
         rows_all[d, NE:ROWS, q * 512 : (q + 1) * 512] = got.astype(BF16)
 
+    def block_part(block, half):
+        part = rows_all.at[block]
+        return part if half is None else part.at[:, half * 1024 : (half + 1) * 1024]
+
     def gather(block, kind, to_dp, half=None):
-        part = rows_all.at[block]
-        if half is not None:
-            part = part.at[:, half * 1024 : (half + 1) * 1024]
+        part = block_part(block, half)
         return pltpu.make_async_remote_copy(
             src_ref=part,
             dst_ref=part,
@@ -302,17 +304,23 @@
         )
 
     ahead, behind, far = same_core(1), same_core(3), same_core(2)
-    FROM_BEHIND, FROM_AHEAD, FROM_FAR, FROM_PARTNER = range(4)
-    gather(d, FROM_BEHIND, ahead).start()
-    gather(d, FROM_AHEAD, behind).start()
+    FROM_FAR, FROM_PARTNER = 4, 5
+    gather(d, 0, ahead, 1).start()
+    gather(d, 1, behind, 0).start()
+    gather(d, 2, ahead, 0).start()
+    gather(d, 3, behind, 1).start()
     gather(d, FROM_PARTNER, partner).start()
 
+    def gather_pass():
+        wait_bytes(block_part(behind, 1), grecv.at[0])
+        gather(behind, FROM_FAR, ahead, 1).start()
+        wait_bytes(block_part(ahead, 0), grecv.at[1])
+        gather(ahead, FROM_FAR, behind, 0).start()
+
     def gather_near():
-        wait_bytes(rows_all.at[behind], grecv.at[FROM_BEHIND])
-        gather(behind, FROM_FAR, ahead, 1).start()
+        wait_bytes(block_part(behind, 0), grecv.at[2])
         gather(behind, FROM_PARTNER, partner).start()
-        wait_bytes(rows_all.at[ahead], grecv.at[FROM_AHEAD])
-        gather(ahead, FROM_FAR, behind, 0).start()
+        wait_bytes(block_part(ahead, 1), grecv.at[3])
         gather(ahead, FROM_PARTNER, partner).start()
 
     def gather_far():
@@ -326,6 +334,7 @@
         dout_send[:, c * 256 : (c + 1) * 256] = part.astype(BF16)
     exchange(*DOUT)
 
+    gather_pass()
     arrive(*QKV)
 
     def late(wide, part):
@@ -428,7 +437,6 @@
     parts = [part.reshape(N, NL, E) for part in (dquery, dkey, dvalue)]
     parts.append(jnp.zeros((N, 8, E), F32))
     dqkv_send[:, 3 * NE : GRAD_ROWS, :] = jnp.concatenate(parts, axis=1).astype(BF16)
-    exchange(*GRAD_LATE)
     gather_far()
 
     wait_bytes(att_recv, recv.at[ATT])
@@ -468,6 +476,7 @@
                             sum1_send[1, j, 2 * p + i, :, cut] = part[i, j]
         for i in (2, 1, 3):
             sum_copy(half, 0, i).start()
+    exchange(*GRAD_LATE)
     exchange(*GRAD_Q)
     for half in range(2):
         wait_bytes(sum1_recv.at[half], sum_recv.at[0, half])
@@ -502,6 +511,10 @@
         writes.append(pltpu.make_async_copy(source, target, local_sem.at[len(writes)]))
         writes[-1].start()
 
+    arrive(*GRAD_V)
+    arrive(*GRAD_K)
+    dkve_v[0] = jnp.stack([out[NE : 2 * NE], out[2 * NE : 3 * NE]], axis=1)
+    write(dkve_v, dkeyval_early)
     arrive(*GRAD_LATE)
     for c in range(4):
         cut = slice(c * 512, (c + 1) * 512)
@@ -512,10 +525,6 @@
         )
     write(dql_v, dquery_late)
     write(dkvl_v, dkeyval_late)
-    arrive(*GRAD_V)
-    arrive(*GRAD_K)
-    dkve_v[0] = jnp.stack([out[NE : 2 * NE], out[2 * NE : 3 * NE]], axis=1)
-    write(dkve_v, dkeyval_early)
     for grad, (first, last) in (
         (GRAD_Q, (0, NE)),
         (GRAD_LATE, (3 * NE, GRAD_ROWS)),
@@ -609,7 +618,7 @@
             pltpu.SemaphoreType.DMA((9,)),
             pltpu.SemaphoreType.DMA((9,)),
             pltpu.SemaphoreType.DMA,
-            pltpu.SemaphoreType.DMA((4,)),
+            pltpu.SemaphoreType.DMA((6,)),
             pltpu.SemaphoreType.DMA((2,)),
             pltpu.SemaphoreType.DMA((2, 2)),
         ],

time: 62 us -> 60.4 us (0.974)
  Pallas kernels: 61.3 us -> 59.6 us
    pallas_call x1, Pallas kernels: 59.1 us -> 57.5 us  [shards(): pl.pallas_call(kernel, out_shape=between, in_specs=[hbm] * 8, out_specs=(...]
where the time goes in v7:
time: 60.4 us; the launch traced here: 60.3 us
  Pallas kernels  59.6 us (99%)
  between operations  0.64 us (1%)
    pallas_call x1, Pallas kernels, shards(): pl.pallas_call(kernel, out_shape=between, in_specs=[hbm] * 8, out_specs=(...  57.5 us
    pallas_call x1, Pallas kernels, shards(): pl.pallas_call(finish, out_shape=results, in_specs=[hbm] * 5, out_specs=(...  2.12 us

profile of v7, /device:TPU:0, one launch (start us, length us, event | category | flops | bytes accessed | tf_op | source)
XLA Modules:
  0.0 60.3 jit_solution(873503031019512749)
XLA Ops:
  0.6 57.5 %rows_attention_weight.1 = (bf16[1,48,2048]{2,1,0:T(8,128)(2,1)}, bf16[1,48,2,2048]{3,2,1,0:T(2,128)(2,1)}, bf16[1,24,2048]{2,1,0:T(8,128)(2,1)}, bf16[1,24,2,20...) custom-call(s32[1,256]{1,0:T(1,128)} %depths.1, s32[2,1,256]{2,1,0:T(1,128)} %owners.1, bf16[2,1,256,2048]{3,2,1,0:T(8,128)(2,1)} %cot.1, ...), custom_call_target="tpu_custom_call" | custom-call | flops 3000000000 | bytes 20000000 | tf_op jit(solution)/shard_map/rows_attention_weight/pallas_call | solution.py:579
  58.2 2.1 %outputs.1 = (bf16[1,48,2048]{2,1,0:T(8,128)(2,1)}, bf16[1,48,2,2048]{3,2,1,0:T(2,128)(2,1)}, bf16[1,24,2048]{2,1,0:T(8,128)(2,1)}, bf16[1,24,2,2048]{3,2,1,0:T(2,128)(2,1)}, f32[16,2048]{1,0:T(8,128)}) custom-call(bf16[1,48,2048]{2,1,0:T(8,128)(2,1)} %get-tuple-element.10.refs_0_, bf16[1,48,2,2048]{3,2,1,0:T(2,128)(2,1)} %get-tuple-element.11.refs_1_, ...), custom_call_target="tpu_custom_call" | custom-call | tf_op jit(solution)/shard_map/outputs/pallas_call | solution.py:636

commit v8 on v7

--- a/solution.py
+++ b/solution.py
@@ -24,6 +24,7 @@
 )
 KE, KL = N * NE, N * NL
 SCALE = E**-0.5
+LOG2_E = 1.4426950408889634
 
 
 def dot(a, b):
@@ -65,7 +66,7 @@
     z, y = lax.div(s, 4), lax.rem(s, 4)
 
     def head_of(j):
-        return lax.rem(chip + lax.div(j, 4) + 2 * core, 4) * 4 + lax.rem(j, 4)
+        return lax.rem(chip + lax.rem(j, 4) + 2 * core, 4) * 4 + lax.div(j, 4)
 
     def same_core(i):
         return lax.rem(chip + i, 4) * 2 + core
@@ -109,7 +110,7 @@
     for from_dp in range(DP):
         turn = lax.rem(chip + 8 - from_dp // 2 - 2 * (from_dp % 2), 4)
         for p in range(2):
-            from_seq = turn * 4 + 2 * core + p
+            from_seq = (2 * core + p) * 4 + turn
 
             @pl.when(jnp.logical_or(d != from_dp, from_seq != s))
             def _(from_dp=from_dp, from_seq=from_seq):
@@ -341,11 +342,11 @@
         return wide[:, part * NL : (part + 1) * NL].reshape(KL, E)
 
     def softmax(query, key, value, row, col):
-        scores = dot_nt(query, key) * SCALE
+        scores = dot_nt(query, key) * (SCALE * LOG2_E)
         scores = jnp.where(row <= col, scores, -1e30)
         top = jnp.max(scores, axis=1, keepdims=True)
-        weights = jnp.exp(scores - top)
-        probs = weights / jnp.sum(weights, axis=1, keepdims=True)
+        weights = jnp.exp2(scores - top)
+        probs = weights * (1.0 / jnp.sum(weights, axis=1, keepdims=True))
         probs_bf = probs.astype(BF16)
         return probs, probs_bf, dot(probs_bf, value)
 
@@ -437,6 +438,7 @@
     parts = [part.reshape(N, NL, E) for part in (dquery, dkey, dvalue)]
     parts.append(jnp.zeros((N, 8, E), F32))
     dqkv_send[:, 3 * NE : GRAD_ROWS, :] = jnp.concatenate(parts, axis=1).astype(BF16)
+    exchange(*GRAD_Q)
     gather_far()
 
     wait_bytes(att_recv, recv.at[ATT])
@@ -477,7 +479,6 @@
         for i in (2, 1, 3):
             sum_copy(half, 0, i).start()
     exchange(*GRAD_LATE)
-    exchange(*GRAD_Q)
     for half in range(2):
         wait_bytes(sum1_recv.at[half], sum_recv.at[0, half])
         total = sum1_send[half, z if half == 0 else y].astype(F32)
@@ -542,7 +543,7 @@
 
 def finish(*refs):
     sources, targets, held, dw_v, sem = refs[0:5], refs[5:10], refs[10:15], refs[15], refs[16]
-    order = (4, 1, 3, 0, 2)
+    order = (1, 4, 3, 0, 2)
     loads = {i: pltpu.make_async_copy(sources[i], held[i], sem.at[i]) for i in order}
     stores = {
         i: pltpu.make_async_copy(dw_v if i == 4 else held[i], targets[i], sem.at[5 + i])

time: 60.4 us -> 60.3 us (level); the launches traced: 60.3 us -> 59.2 us
  Pallas kernels: 59.6 us -> 58.5 us
    pallas_call x1, Pallas kernels: 57.5 us -> 56.5 us  [shards(): pl.pallas_call(kernel, out_shape=between, in_specs=[hbm] * 8, out_specs=(...]
where the time goes in v8:
time: 60.3 us; the launch traced here: 59.2 us
  Pallas kernels  58.5 us (97%)
  between operations  0.64 us (1%)
    pallas_call x1, Pallas kernels, shards(): pl.pallas_call(kernel, out_shape=between, in_specs=[hbm] * 8, out_specs=(...  56.5 us
    pallas_call x1, Pallas kernels, shards(): pl.pallas_call(finish, out_shape=results, in_specs=[hbm] * 5, out_specs=(...  2.04 us

profile of v8, /device:TPU:0, one launch (start us, length us, event | category | flops | bytes accessed | tf_op | source)
XLA Modules:
  0.0 59.2 jit_solution(12736439514655962240)
XLA Ops:
  0.6 56.5 %rows_attention_weight.1 = (bf16[1,48,2048]{2,1,0:T(8,128)(2,1)}, bf16[1,48,2,2048]{3,2,1,0:T(2,128)(2,1)}, bf16[1,24,2048]{2,1,0:T(8,128)(2,1)}, bf16[1,24,2,20...) custom-call(s32[1,256]{1,0:T(1,128)} %depths.1, s32[2,1,256]{2,1,0:T(1,128)} %owners.1, bf16[2,1,256,2048]{3,2,1,0:T(8,128)(2,1)} %cot.1, ...), custom_call_target="tpu_custom_call" | custom-call | flops 3000000000 | bytes 20000000 | tf_op jit(solution)/shard_map/rows_attention_weight/pallas_call | solution.py:580
  57.2 2.0 %outputs.1 = (bf16[1,48,2048]{2,1,0:T(8,128)(2,1)}, bf16[1,48,2,2048]{3,2,1,0:T(2,128)(2,1)}, bf16[1,24,2048]{2,1,0:T(8,128)(2,1)}, bf16[1,24,2,2048]{3,2,1,0:T(2,128)(2,1)}, f32[16,2048]{1,0:T(8,128)}) custom-call(bf16[1,48,2048]{2,1,0:T(8,128)(2,1)} %get-tuple-element.10.refs_0_, bf16[1,48,2,2048]{3,2,1,0:T(2,128)(2,1)} %get-tuple-element.11.refs_1_, ...), custom_call_target="tpu_custom_call" | custom-call | tf_op jit(solution)/shard_map/outputs/pallas_call | solution.py:637
